TPU v7x, 256 devices: a whole 4x4x8 slice. The times are simulated.
256 devices in a mesh: leaf: 16 (over x_lo, z), row: 4 (over x_hi, core), col: 4 (over y).
Axes of the slice: x: 4 (x_hi: 2, x_lo: 2; x = x_hi * 2 + x_lo), y: 4, z: 8, core: 2. Of those that a mesh axis runs over, the one named last changes fastest.
Arguments:
- leaf_front: float32 [16, 7, 4, 128, 7, 4, 128], P('leaf', None, 'row', None, None, 'col')
- leaf_pattern: int32 [16, 28, 28], P('leaf'), may hold values from 0 to 1, as said below
- parent_panel: float32 [2, 16, 7, 4, 128, 4, 128], P(None, 'leaf', None, 'row', None, 'col'), may hold values from -0.125 to 0.125
- parent_diag: float32 [2, 16, 7, 4, 128], P(None, 'leaf', None, 'row'), may hold values from 1.5 to 2.5
- parent_pattern: int32 [2, 16, 28, 28], replicated, may hold values from 0 to 1, as said below
- ext_map: int32 [2, 16, 24], replicated, may hold values from 0 to 27, as said below
Outputs:
- panels: float32 [3, 16, 7, 4, 128, 4, 128], P(None, 'leaf', None, 'row', None, 'col')
- top_update: float32 [16, 6, 4, 128, 6, 4, 128], P('leaf', None, 'row', None, None, 'col')
Inputs may be any that keep to these rules, and one draw needn't show every extreme that they name: leaf_pattern: symmetric, with every diagonal block 1. parent_pattern: symmetric, with every diagonal block 1. parent_pattern[d, n] belongs to node n at depth d+1; rows n of 16 / 2^(d+1) or more are not read. ext_map[d, n] belongs to node n at depth d; rows n of 16 / 2^d or more are not read. Along its 24 entries it rises strictly; ext_map[d, n, j] - j is the same for the 4 entries j of each aligned run of 4, never falls and lies in 0 to 4. Among the entries j of one class of j mod 4, at most two lie in one class of ext_map mod 4, and in every row some two do.
All inputs are finite; a program needn't handle non-finite values.
Results may differ from a plain program's by a relative error of at most 0.0003.
Values sent between devices are 32-bit elements; how exact they have to be, the bound alone decides.
No kernel may reach another device: no remote copies, remote signals or barrier semaphores. Data moves between devices by JAX's collectives and lax.ppermute only.
A program may use at most 128 MiB of HBM per device.

v0:
```python
import jax
import jax.numpy as jnp
from jax import lax
from jax.sharding import PartitionSpec as P

highest = lax.Precision.HIGHEST
slot_limit = 2


def in_order(blocks, dim):
    dims = list(blocks.shape[1:])
    dims[dim] *= blocks.shape[0]
    return jnp.moveaxis(blocks, 0, dim).reshape(dims)


def copy_for_each(array, axis):
    copies = jnp.broadcast_to(array, (lax.axis_size(axis), *array.shape))
    return lax.all_to_all(copies, axis, split_axis=0, concat_axis=0, tiled=True)


def gathered_copies(array, axis, dim):
    return in_order(copy_for_each(array, axis), dim)


def from_root(array, axis, root):
    return lax.dynamic_index_in_dim(lax.all_gather(array, axis), root, 0, keepdims=False)


def partner(block, axis, bit):
    count = lax.axis_size(axis)
    route = []
    for low in range(count):
        high = low | 1 << bit
        if high != low and high < count:
            route += [(low, high), (high, low)]
    return lax.ppermute(block, axis, route)


def symmetric_lower(matrix):
    return jnp.tril(matrix) + jnp.tril(matrix, -1).T


def local_mask(pattern, my_row, my_col, block_rows, grid_side):
    layout = pattern.reshape(block_rows, grid_side, block_rows, grid_side).astype(jnp.float32)
    picked = lax.dynamic_index_in_dim(layout, my_row, 1, keepdims=False)
    picked = lax.dynamic_index_in_dim(picked, my_col, 2, keepdims=False)
    return picked[:, None, :, None]


def factor_whole(front_local, my_row, my_col, grid_side, block_size, kept):
    local_order = front_local.shape[0]
    block_rows = local_order // block_size
    pivots = grid_side * block_size
    squares = gathered_copies(front_local[None, :block_size, :block_size], ("row", "col"), 0)
    corner = (
        squares.reshape(grid_side, grid_side, block_size, block_size)
        .transpose(0, 2, 1, 3)
        .reshape(pivots, pivots)
    )
    pivot_wide = lax.all_gather(front_local[:, :block_size], "col", axis=1, tiled=True)
    pivot_factor = jnp.linalg.cholesky(symmetric_lower(corner))
    solved = lax.linalg.triangular_solve(
        pivot_factor, pivot_wide[block_size:], left_side=False, lower=True, transpose_a=True
    )
    top_rows = lax.dynamic_slice(pivot_factor, (my_row * block_size, 0), (block_size, pivots))
    rows_here = jnp.concatenate([top_rows, solved], axis=0)
    rows_there = from_root(rows_here, "row", my_col)
    picked_rows = jnp.take(
        rows_there.reshape(block_rows, block_size, pivots), kept, axis=0
    ).reshape(-1, pivots)
    panel_col = lax.dynamic_slice(rows_here, (0, my_col * block_size), (local_order, block_size))
    update = front_local[block_size:, block_size:] - jnp.einsum(
        "ik,jk->ij",
        rows_here[block_size:],
        picked_rows[block_size:],
        precision=highest,
        preferred_element_type=jnp.float32,
    )
    return (panel_col, update)


def factor(front_local, my_row, my_col, grid_side, block_size, kept):
    return factor_whole(front_local, my_row, my_col, grid_side, block_size, kept)


def route_tables(child_map, grid_side, my_index, block_rows):
    layout = child_map.reshape(-1, grid_side)
    row_total = layout.shape[0]
    target = layout % grid_side
    home_row = layout // grid_side
    order_ids = jnp.arange(row_total)
    before = order_ids[:, None] > order_ids[None, :]
    shared = target[:, None, :] == target[None, :, :]
    position = jnp.sum(jnp.logical_and(shared, before[:, :, None]).astype(jnp.int32), axis=1)
    own_target = lax.dynamic_index_in_dim(target, my_index, 1, keepdims=False)
    own_position = lax.dynamic_index_in_dim(position, my_index, 1, keepdims=False)
    slot_ids = jnp.arange(slot_limit)
    side_ids = jnp.arange(grid_side)
    outgoing = jnp.logical_and(
        own_target[None, None, :] == side_ids[:, None, None],
        own_position[None, None, :] == slot_ids[None, :, None],
    ).astype(jnp.int32)
    send_index = jnp.sum(outgoing * order_ids[None, None, :], axis=2).reshape(-1)
    send_valid = jnp.sum(outgoing, axis=2).reshape(-1).astype(jnp.float32)
    matches = (
        (target == my_index)[:, :, None, None]
        & (position[:, :, None, None] == slot_ids[None, None, :, None])
        & (home_row[:, :, None, None] == jnp.arange(block_rows)[None, None, None, :])
    )
    incoming = jnp.sum(matches.astype(jnp.int32), axis=0)
    flat_ids = side_ids[:, None] * slot_limit + slot_ids[None, :]
    place_index = jnp.sum(incoming * flat_ids[:, :, None], axis=(0, 1))
    place_valid = jnp.sum(incoming, axis=(0, 1)).astype(jnp.float32)
    return (send_index, send_valid, place_index, place_valid)


def shards(leaf_front, leaf_pattern, parent_panel, parent_diag, parent_pattern, ext_map):
    block_rows = leaf_front.shape[1]
    block_size = leaf_front.shape[3]
    local_order = block_rows * block_size
    contrib_rows = block_rows - 1
    half_cols = contrib_rows // 2
    levels = parent_panel.shape[0]
    grid_side = lax.axis_size("row")
    my_row = lax.axis_index("row")
    my_col = lax.axis_index("col")
    my_leaf = lax.axis_index("leaf")
    all_blocks = jnp.arange(block_rows, dtype=jnp.int32)
    leaf_local = leaf_front[0, :, 0, :, :, 0, :]
    front_local = (
        leaf_local * local_mask(leaf_pattern[0], my_row, my_col, block_rows, grid_side)
    ).reshape(local_order, local_order)
    panel_col, update = factor(front_local, my_row, my_col, grid_side, block_size, all_blocks)
    panel_list = [panel_col]
    acc_panel = parent_panel.reshape(levels, block_rows, block_size, block_size)
    acc_diag = parent_diag.reshape(levels, block_rows, block_size)
    block_same = (
        jnp.arange(block_rows)[:, None, None, None] == jnp.arange(block_rows)[None, None, :, None]
    )
    element_same = (
        jnp.arange(block_size)[None, :, None, None] == jnp.arange(block_size)[None, None, None, :]
    )
    diag_spots = jnp.logical_and(jnp.logical_and(block_same, element_same), my_row == my_col)
    for depth in range(levels):
        child_node = jnp.right_shift(my_leaf, depth)
        child_map = lax.dynamic_index_in_dim(ext_map[depth], child_node, 0, keepdims=False)
        row_src, row_ok, row_place, row_in = route_tables(child_map, grid_side, my_row, block_rows)
        col_src, col_ok, col_place, col_in = route_tables(child_map, grid_side, my_col, block_rows)
        update_blocks = update.reshape(contrib_rows, block_size, contrib_rows, block_size)
        rows_taken = jnp.take(update_blocks, row_src, axis=0) * row_ok[:, None, None, None]
        packed = jnp.take(rows_taken, col_src, axis=2) * col_ok[None, None, :, None]
        packed = packed.reshape(
            grid_side, slot_limit, block_size, grid_side, slot_limit, block_size
        )
        packed = packed.transpose(0, 3, 1, 4, 2, 5).reshape(
            grid_side * grid_side, slot_limit * slot_limit, block_size, block_size
        )
        received = lax.all_to_all(packed, ("row", "col"), split_axis=0, concat_axis=0, tiled=True)
        received = received.reshape(
            grid_side, grid_side, slot_limit, slot_limit, block_size, block_size
        )
        received = received.transpose(0, 2, 1, 3, 4, 5).reshape(
            grid_side * slot_limit, grid_side * slot_limit, block_size, block_size
        )
        placed = jnp.take(received, row_place, axis=0)
        placed = jnp.take(placed, col_place, axis=1)
        placed = placed * (row_in[:, None, None, None] * col_in[None, :, None, None])
        spread = placed.transpose(0, 2, 1, 3)
        parent_node = jnp.right_shift(my_leaf, depth + 1)
        pattern = lax.dynamic_index_in_dim(parent_pattern[depth], parent_node, 0, keepdims=False)
        mask_here = local_mask(pattern, my_row, my_col, block_rows, grid_side)
        own_front = spread + jnp.where(
            diag_spots, acc_diag[depth][:, :, None, None] * mask_here, 0.0
        )
        own_front = own_front.at[:, :, 0, :].add(mask_here[:, :, 0, :] * acc_panel[depth])
        side_bit = jnp.right_shift(my_leaf, depth) % 2
        keep_start = 1 + half_cols * side_bit
        give_start = 1 + half_cols * (1 - side_bit)
        first_cols = own_front[:, :, :1, :]
        mine = lax.dynamic_slice_in_dim(own_front, keep_start, half_cols, 2)
        given = lax.dynamic_slice_in_dim(own_front, give_start, half_cols, 2)
        if depth + 1 < levels:
            partner_first, partner_part, partner_panel, partner_diag = partner(
                (first_cols, given, acc_panel[depth + 1 :], acc_diag[depth + 1 :]), "leaf", depth
            )
            acc_panel = jnp.concatenate(
                [acc_panel[: depth + 1], acc_panel[depth + 1 :] + partner_panel], axis=0
            )
            acc_diag = jnp.concatenate(
                [acc_diag[: depth + 1], acc_diag[depth + 1 :] + partner_diag], axis=0
            )
        else:
            partner_first, partner_part = partner((first_cols, given), "leaf", depth)
        merged = jnp.concatenate([first_cols + partner_first, mine + partner_part], axis=2)
        merged = merged.reshape(local_order, (1 + half_cols) * block_size)
        kept = jnp.concatenate([jnp.zeros((1,), jnp.int32), keep_start + jnp.arange(half_cols)])
        panel_col, part_update = factor(merged, my_row, my_col, grid_side, block_size, kept)
        other_part = partner(part_update, "leaf", depth)
        update = jnp.where(
            side_bit == 0,
            jnp.concatenate([part_update, other_part], axis=1),
            jnp.concatenate([other_part, part_update], axis=1),
        )
        panel_list.append(panel_col)
    panels = jnp.stack(panel_list).reshape(levels + 1, 1, block_rows, 1, block_size, 1, block_size)
    element_ids = jnp.arange(block_size)
    row_ids = (grid_side * (jnp.arange(contrib_rows) + 1) + my_row)[
        :, None
    ] * block_size + element_ids[None, :]
    col_ids = (grid_side * (jnp.arange(contrib_rows) + 1) + my_col)[
        :, None
    ] * block_size + element_ids[None, :]
    keep_lower = row_ids[:, :, None, None] >= col_ids[None, None, :, :]
    top_rows = jnp.where(
        keep_lower, update.reshape(contrib_rows, block_size, contrib_rows, block_size), 0.0
    )
    top_update = top_rows.reshape(1, contrib_rows, 1, block_size, contrib_rows, 1, block_size)
    return (panels, top_update)


def solution(mesh):
    return jax.shard_map(
        shards,
        mesh=mesh,
        in_specs=(
            P("leaf", None, "row", None, None, "col", None),
            P("leaf", None, None),
            P(None, "leaf", None, "row", None, "col", None),
            P(None, "leaf", None, "row", None),
            P(),
            P(),
        ),
        out_specs=(
            P(None, "leaf", None, "row", None, "col", None),
            P("leaf", None, "row", None, None, "col", None),
        ),
        check_vma=False,
    )
```

profile of v0, /device:TPU:1, one launch (start us, length us, event | category | flops | bytes accessed | tf_op | source)
XLA Modules:
  0.0 1199.3 jit_solution(11883400671864180489)
XLA Ops:
  10.0 11.4 reduce.24
  27.0 8.4 all-to-all-start
  36.6 15.7 %all-to-all-done = f32[16,1,128,128]{3,2,1,0:T(8,128)} async-done(((f32[16,1,128,128]{3,2,1,0:T(8,128)}), f32[16,1,128,128]{3,2,1,0:T(8,128)}, u32[]{:S(2)}, u32[]{:S(2)}) %all-to-all-start) | async-done | bytes 1048608 | tf_op jit(solution)/shard_map/all_to_all | solution.py:18
  55.6 11.7 cholesky.374
  67.4 9.8 custom-call.31
  78.2 12.1 %cholesky.393 = f32[128,128]{1,0:T(8,128)S(1)} custom-call(f32[128,128]{1,0:T(8,128)S(1)} %copy.277), custom_call_target="Cholesky" | custom-call | tf_op jit(solution)/shard_map/jit(cholesky)/cholesky | solution.py:61
  90.4 9.8 custom-call.32
  101.1 11.7 cholesky.414
  112.9 9.8 custom-call.33
  123.5 11.9 cholesky.431
  140.9 8.0 while.8
  148.9 39.3 %custom-call.34 = f32[4,128,128]{1,2,0:T(8,128)S(1)} custom-call(f32[4,128,128]{2,1,0:T(8,128)S(1)} %get-tuple-element.53), custom_call_target="InvertDiagBlocksLowerTriangular" | custom-call | tf_op jit(solution)/shard_map/triangular_solve/custom-call.3 | solution.py:62
  195.2 3.1 convolution_subtract_fusion.4
  208.6 51.7 %all-gather.16.cloned.1.call-done = f32[3584,512]{0,1:T(8,128)} async-done(((f32[896,512]{0,1:T(8,128)}), f32[3584,512]{0,1:T(8,128)}) %all-gather.16.cloned.1.call-update) | async-done | bytes 7340048 | tf_op jit(solution)/shard_map/all_gather | solution.py:26
  260.3 8.7 copy.340
  274.4 9.2 slice_subtract_fusion
  292.6 2.9 gather_fusion.2
  300.5 4.6 all-to-all-start.1
  308.8 44.9 %all-to-all-done.1 = f32[16,4,128,128]{3,2,1,0:T(8,128)} async-done(((f32[16,4,128,128]{3,2,1,0:T(8,128)}), f32[16,4,128,128]{3,2,1,0:T(8,128)}, u32[]{:S(2)}, u32[]{:S(2)}) %all-to-all-start.1) | async-done | bytes 4194336 | tf_op jit(solution)/shard_map/all_to_all | solution.py:158
  353.6 4.7 copy.292
  358.3 4.8 gather_fusion.3
  363.1 4.4 broadcast_select_fusion.1
  367.4 2.8 gather_fusion.4
  374.5 7.6 collective-permute-done
  385.7 26.3 %collective-permute-done.1 = f32[7,128,3,128]{3,1,0,2:T(8,128)S(1)} collective-permute-done((f32[7,128,3,128]{3,1,0,2:T(8,128)S(1)}, f32[7,128,3,128]{3,1,0,2:T(8,128)S(1)}, u32[]{:S(2)}, u32[]{:S(2)}) %collective-permute-start.1) | collective-permute-done | bytes 1376288 | tf_op jit(solution)/shard_map/ppermute | solution.py:36
  416.3 16.8 %all-to-all-start.2 = ((f32[16,1,128,128]{3,2,1,0:T(8,128)}), f32[16,1,128,128]{3,2,1,0:T(8,128)S(1)}, u32[]{:S(2)}, u32[]{:S(2)}) async-start(f32[16,1,128,128]{3,2,1,0:T(8,128)} %broadcast_in_dim.96), calls=%async_computation.2 | async-start | bytes 2097152 | tf_op jit(solution)/shard_map/all_to_all | solution.py:18
  434.2 15.6 %all-to-all-done.2 = f32[16,1,128,128]{3,2,1,0:T(8,128)S(1)} async-done(((f32[16,1,128,128]{3,2,1,0:T(8,128)}), f32[16,1,128,128]{3,2,1,0:T(8,128)S(1)}, u32[]{:S(2)}, u32[]{:S(2)}) %all-to-all-start.2) | async-done | bytes 1048608 | tf_op jit(solution)/shard_map/all_to_all | solution.py:18
  451.8 11.7 cholesky.446
  463.6 9.8 custom-call.35
  474.5 11.7 cholesky.465
  486.2 10.0 custom-call.36
  497.1 11.7 cholesky.486
  508.9 9.8 custom-call.37
  519.5 12.2 %cholesky.503 = f32[128,128]{1,0:T(8,128)S(1)} custom-call(f32[128,128]{1,0:T(8,128)S(1)} %copy.306), custom_call_target="Cholesky" | custom-call | tf_op jit(solution)/shard_map/jit(cholesky)/cholesky | solution.py:61
  537.1 7.7 while.9
  544.7 39.3 %custom-call.38 = f32[4,128,128]{1,2,0:T(8,128)S(1)} custom-call(f32[4,128,128]{2,1,0:T(8,128)S(1)} %get-tuple-element.54), custom_call_target="InvertDiagBlocksLowerTriangular" | custom-call | tf_op jit(solution)/shard_map/triangular_solve/custom-call.3 | solution.py:62
  591.1 3.1 convolution_subtract_fusion.2
  603.5 51.9 %all-gather.18.cloned.1.call-done = f32[3584,512]{0,1:T(8,128)} async-done(((f32[896,512]{0,1:T(8,128)}), f32[3584,512]{0,1:T(8,128)}) %all-gather.18.cloned.1.call-update) | async-done | bytes 7340048 | tf_op jit(solution)/shard_map/all_gather | solution.py:26
  655.5 8.5 copy.342
  675.6 22.8 %collective-permute-done.2 = f32[768,384]{0,1:T(8,128)S(1)} collective-permute-done((f32[768,384]{0,1:T(8,128)S(1)}, f32[768,384]{0,1:T(8,128)S(1)}, u32[]{:S(2)}, u32[]{:S(2)}) %collective-permute-start.2) | collective-permute-done | bytes 1179680 | tf_op jit(solution)/shard_map/ppermute | solution.py:36
  709.2 2.7 gather_fusion.7
  717.0 5.5 all-to-all-start.3
  726.6 44.5 %all-to-all-done.3 = f32[16,4,128,128]{3,2,1,0:T(8,128)} async-done(((f32[16,4,128,128]{3,2,1,0:T(8,128)}), f32[16,4,128,128]{3,2,1,0:T(8,128)}, u32[]{:S(2)}, u32[]{:S(2)}) %all-to-all-start.3) | async-done | bytes 4194336 | tf_op jit(solution)/shard_map/all_to_all | solution.py:158
  771.1 4.7 copy.319
  775.7 4.8 gather_fusion.8
  780.5 4.4 broadcast_select_fusion
  784.9 2.8 gather_fusion.9
  794.4 78.8 %collective-permute-done.5 = f32[7,128,1,128]{3,1,0,2:T(8,128)} collective-permute-done((f32[7,128,1,128]{3,1,0,2:T(8,128)S(1)}, f32[7,128,1,128]{3,1,0,2:T(8,128)}, u32[]{:S(2)}, u32[]{:S(2)}) %collective-permute-start.5) | collective-permute-done | bytes 458784 | tf_op jit(solution)/shard_map/ppermute | solution.py:36
  878.5 11.1 all-to-all-start.4
  891.5 14.8 %all-to-all-done.4 = f32[16,1,128,128]{3,2,1,0:T(8,128)S(1)} async-done(((f32[16,1,128,128]{3,2,1,0:T(8,128)}), f32[16,1,128,128]{3,2,1,0:T(8,128)S(1)}, u32[]{:S(2)}, u32[]{:S(2)}) %all-to-all-start.4) | async-done | bytes 1048608 | tf_op jit(solution)/shard_map/all_to_all | solution.py:18
  908.3 11.7 cholesky.518
  920.2 9.8 custom-call.39
  930.7 11.9 cholesky.537
  942.6 9.8 custom-call.40
  953.1 11.7 cholesky.558
  964.8 9.8 custom-call.41
  975.2 11.7 cholesky.575
  992.4 8.2 while.10
  1000.6 39.3 %custom-call.42 = f32[4,128,128]{1,2,0:T(8,128)S(1)} custom-call(f32[4,128,128]{2,1,0:T(8,128)S(1)} %get-tuple-element.55), custom_call_target="InvertDiagBlocksLowerTriangular" | custom-call | tf_op jit(solution)/shard_map/triangular_solve/custom-call.3 | solution.py:62
  1046.9 3.1 convolution_subtract_fusion
  1058.0 53.4 %all-gather.20.cloned.1.call-done = f32[3584,512]{0,1:T(8,128)} async-done(((f32[896,512]{0,1:T(8,128)}), f32[3584,512]{0,1:T(8,128)}) %all-gather.20.cloned.1.call-update) | async-done | bytes 7340048 | tf_op jit(solution)/shard_map/all_gather | solution.py:26
  1111.3 8.4 copy.346
  1138.1 42.6 %collective-permute-done.7 = f32[768,384]{0,1:T(8,128)} collective-permute-done((f32[768,384]{0,1:T(8,128)S(1)}, f32[768,384]{0,1:T(8,128)}, u32[]{:S(2)}, u32[]{:S(2)}) %collective-permute-start.7) | collective-permute-done | bytes 1179680 | tf_op jit(solution)/shard_map/ppermute | solution.py:36
  1188.2 3.8 copy.333
  (484 shorter events, 211.4 us)
Async XLA Ops:
  10.0 11.4 copy-start.21
  22.1 2.0 copy-start
  25.7 10.5 copy-start.3
  27.0 25.3 %all-to-all-start = ((f32[16,1,128,128]{3,2,1,0:T(8,128)}), f32[16,1,128,128]{3,2,1,0:T(8,128)}, u32[]{:S(2)}, u32[]{:S(2)}) async-start(f32[16,1,128,128]{3,2,1,0:T(8,128)} %broadcast_in_dim.86), calls=%async_computation | async-start | bytes 2097152 | tf_op jit(solution)/shard_map/all_to_all | solution.py:18
  35.4 153.0 %all-gather.10.cloned.1.call-start = ((), (), s32[]{:S(2)}) async-start(), calls=%async_computation.5 | async-start | bytes 2293760 | tf_op jit(solution)/shard_map/all_gather | solution.py:60
  36.3 224.0 %all-gather.16.cloned.1.call-start = ((), (), s32[]{:S(2)}) async-start(), calls=%async_computation.8 | async-start | bytes 9175040 | tf_op jit(solution)/shard_map/all_gather | solution.py:26
  36.6 18.1 %copy-start.31 = (s32[512]{0:T(512)}, s32[512]{0:T(512)S(1)}, u32[]{:S(2)}) copy-start(s32[512]{0:T(512)S(1)} %iota_add_fusion.2) | copy-start | bytes 6148
  188.2 6.5 copy-start.19
  202.6 66.4 %copy-start.29 = (s32[6,4]{1,0:T(8,128)}, s32[6,4]{1,0:T(8,128)S(1)}, u32[]{:S(2)}) copy-start(s32[6,4]{1,0:T(8,128)S(1)} %reshape.1010) | copy-start | bytes 292
  203.9 65.1 %copy-start.25 = (s32[6,4]{1,0:T(8,128)}, s32[6,4]{1,0:T(8,128)S(1)}, u32[]{:S(2)}) copy-start(s32[6,4]{1,0:T(8,128)S(1)} %get-tuple-element.95) | copy-start | bytes 292
  287.7 2.6 copy-start.44
  287.8 2.6 copy-start.56
  292.6 2.9 copy-start.41
  292.6 2.9 copy-start.46
  300.4 4.6 copy-start.34
  300.4 5.2 copy-start.24
  300.4 5.3 copy-start.28
  300.4 5.3 copy-start.30
  300.4 5.5 copy-start.26
  300.4 5.5 copy-start.39
  300.5 6.7 copy-start.38
  300.5 53.2 %all-to-all-start.1 = ((f32[16,4,128,128]{3,2,1,0:T(8,128)}), f32[16,4,128,128]{3,2,1,0:T(8,128)}, u32[]{:S(2)}, u32[]{:S(2)}) async-start(f32[16,4,128,128]{3,2,1,0:T(8,128)} %bitcast.287), calls=%async_computation.1 | async-start | bytes 8388608 | tf_op jit(solution)/shard_map/all_to_all | solution.py:158
  307.0 63.2 %copy-start.36 = (pred[7,7]{0,1:T(8,128)(4,1)}, pred[7,7]{0,1:T(8,128)(4,1)S(1)}, u32[]{:S(2)}) copy-start(pred[7,7]{0,1:T(8,128)(4,1)S(1)} %iota_compare_fusion.8) | copy-start | bytes 151
  308.6 61.7 %copy-start.22 = (pred[128,128]{1,0:T(8,128)(4,1)}, pred[128,128]{1,0:T(8,128)(4,1)S(1)}, u32[]{:S(2)}) copy-start(pred[128,128]{1,0:T(8,128)(4,1)S(1)} %iota_compare_fusion.3) | copy-start | bytes 49156
  370.3 2.8 copy-start.15
  373.1 9.0 collective-permute-start
  384.4 27.7 %collective-permute-start.1 = (f32[7,128,3,128]{3,1,0,2:T(8,128)S(1)}, f32[7,128,3,128]{3,1,0,2:T(8,128)S(1)}, u32[]{:S(2)}, u32[]{:S(2)}) collective-permute-start(f32[7,128,3,128]{3,1,0,2:T(8,128)S(1)} %constant_dynamic-slice_fusion.18), channel_id=1, source_target_pairs={{0,16},{16,0},{32,48},{48,32},{64,80},{80,64},{96,112},{112,96},{1... | collective-permute-start | bytes 4128776 | tf_op jit(solution)/shard_map/ppermute | solution.py:36
  415.1 18.9 %copy-start.4 = (f32[112,8,4,128]{3,1,2,0:T(8,128)}, f32[112,8,4,128]{3,1,2,0:T(8,128)S(1)}, u32[]{:S(2)}) copy-start(f32[112,8,4,128]{3,1,2,0:T(8,128)S(1)} %copy.388) | copy-start | bytes 5505028
  416.3 33.5 %all-to-all-start.2 = ((f32[16,1,128,128]{3,2,1,0:T(8,128)}), f32[16,1,128,128]{3,2,1,0:T(8,128)S(1)}, u32[]{:S(2)}, u32[]{:S(2)}) async-start(f32[16,1,128,128]{3,2,1,0:T(8,128)} %broadcast_in_dim.96), calls=%async_computation.2 | async-start | bytes 2097152 | tf_op jit(solution)/shard_map/all_to_all | solution.py:18
  433.0 151.2 %all-gather.12.cloned.1.call-start = ((), (), s32[]{:S(2)}) async-start(), calls=%async_computation.6 | async-start | bytes 2293760 | tf_op jit(solution)/shard_map/all_gather | solution.py:60
  433.9 221.5 %all-gather.18.cloned.1.call-start = ((), (), s32[]{:S(2)}) async-start(), calls=%async_computation.9 | async-start | bytes 9175040 | tf_op jit(solution)/shard_map/all_gather | solution.py:26
  584.1 6.5 copy-start.20
  596.8 2.9 copy-start.5
  668.8 3.6 copy-start.53
  668.8 3.6 copy-start.54
  668.8 3.6 copy-start.55
  671.0 4.6 copy-start.8
  671.0 27.4 %collective-permute-start.2 = (f32[768,384]{0,1:T(8,128)S(1)}, f32[768,384]{0,1:T(8,128)S(1)}, u32[]{:S(2)}, u32[]{:S(2)}) collective-permute-start(f32[768,384]{0,1:T(8,128)S(1)} %fusion.26), channel_id=1, source_target_pairs={{0,16},{16,0},{32,48},{48,32},{64,80},{80,64},{96,112},{112,96},{1... | collective-permute-start | bytes 3538952 | tf_op jit(solution)/shard_map/ppermute | solution.py:36
  704.5 2.4 copy-start.45
  704.5 2.4 copy-start.57
  709.2 2.8 copy-start.42
  709.2 2.8 copy-start.47
  716.9 5.6 copy-start.40
  716.9 6.9 copy-start.16
  716.9 9.0 copy-start.49
  716.9 9.0 copy-start.48
  716.9 9.0 copy-start.51
  716.9 9.1 copy-start.50
  717.0 9.6 copy-start.35
  717.0 54.1 %all-to-all-start.3 = ((f32[16,4,128,128]{3,2,1,0:T(8,128)}), f32[16,4,128,128]{3,2,1,0:T(8,128)}, u32[]{:S(2)}, u32[]{:S(2)}) async-start(f32[16,4,128,128]{3,2,1,0:T(8,128)} %bitcast.288), calls=%async_computation.3 | async-start | bytes 8388608 | tf_op jit(solution)/shard_map/all_to_all | solution.py:158
  722.5 4.0 collective-permute-start.3
  724.6 64.2 %collective-permute-start.4 = (f32[1,7,128,128]{3,2,1,0:T(8,128)}, f32[1,7,128,128]{3,2,1,0:T(8,128)}, u32[]{:S(2)}, u32[]{:S(2)}) collective-permute-start(f32[1,7,128,128]{3,2,1,0:T(8,128)} %slice_bitcast_fusion), channel_id=1, source_target_pairs={{0,16},{16,0},{32,48},{48,32},{64,80},{80,64},{96,112},{112,96},{1... | collective-permute-start | bytes 1376264 | tf_op jit(solution)/shard_map/ppermute | solution.py:36
  784.9 2.8 copy-start.23
  784.9 2.8 copy-start.37
  791.9 82.3 %collective-permute-start.6 = (f32[7,128,3,128]{3,1,0,2:T(8,128)S(1)}, f32[7,128,3,128]{3,1,0,2:T(8,128)S(1)}, u32[]{:S(2)}, u32[]{:S(2)}) collective-permute-start(f32[7,128,3,128]{3,1,0,2:T(8,128)S(1)} %constant_dynamic-slice_fusion.8), channel_id=1, source_target_pairs={{0,32},{32,0},{16,48},{48,16},{64,96},{96,64},{80,112},{112,80},{1... | collective-permute-start | bytes 4128776 | tf_op jit(solution)/shard_map/ppermute | solution.py:36
  794.2 78.9 %collective-permute-start.5 = (f32[7,128,1,128]{3,1,0,2:T(8,128)S(1)}, f32[7,128,1,128]{3,1,0,2:T(8,128)}, u32[]{:S(2)}, u32[]{:S(2)}) collective-permute-start(f32[7,128,1,128]{3,1,0,2:T(8,128)S(1)} %get-tuple-element.129), channel_id=1, source_target_pairs={{0,32},{32,0},{16,48},{48,16},{64,96},{96,64},{80,112},{112,80},{1... | collective-permute-start | bytes 1376264 | tf_op jit(solution)/shard_map/ppermute | solution.py:36
  877.2 12.9 %copy-start.6 = (f32[112,8,4,128]{3,1,2,0:T(8,128)}, f32[112,8,4,128]{3,1,2,0:T(8,128)S(1)}, u32[]{:S(2)}) copy-start(f32[112,8,4,128]{3,1,2,0:T(8,128)S(1)} %copy.387) | copy-start | bytes 5505028
  878.5 27.9 %all-to-all-start.4 = ((f32[16,1,128,128]{3,2,1,0:T(8,128)}), f32[16,1,128,128]{3,2,1,0:T(8,128)S(1)}, u32[]{:S(2)}, u32[]{:S(2)}) async-start(f32[16,1,128,128]{3,2,1,0:T(8,128)} %broadcast_in_dim.101), calls=%async_computation.4 | async-start | bytes 2097152 | tf_op jit(solution)/shard_map/all_to_all | solution.py:18
  889.6 150.5 %all-gather.14.cloned.1.call-start = ((), (), s32[]{:S(2)}) async-start(), calls=%async_computation.7 | async-start | bytes 2293760 | tf_op jit(solution)/shard_map/all_gather | solution.py:60
  891.1 220.3 %all-gather.20.cloned.1.call-start = ((), (), s32[]{:S(2)}) async-start(), calls=%async_computation.10 | async-start | bytes 9175040 | tf_op jit(solution)/shard_map/all_gather | solution.py:26
  1039.9 6.5 copy-start.18
  1126.7 6.8 copy-start.9
  1126.7 53.9 %collective-permute-start.7 = (f32[768,384]{0,1:T(8,128)S(1)}, f32[768,384]{0,1:T(8,128)}, u32[]{:S(2)}, u32[]{:S(2)}) collective-permute-start(f32[768,384]{0,1:T(8,128)S(1)} %fusion.23), channel_id=1, source_target_pairs={{0,32},{32,0},{16,48},{48,16},{64,96},{96,64},{80,112},{112,80},{1... | collective-permute-start | bytes 3538952 | tf_op jit(solution)/shard_map/ppermute | solution.py:36
  1134.6 46.1 %copy-start.10 = (f32[768,384]{0,1:T(8,128)S(1)}, f32[768,384]{0,1:T(8,128)}, u32[]{:S(2)}) copy-start(f32[768,384]{0,1:T(8,128)} %copy-done.9) | copy-start | bytes 3538948
  (13 other events, 16.6 us)
Sparse Core Ops, SparseCore 0:
  38.6 37.2 all-gather.9
  201.2 59.0 all-gather.15
  435.7 36.1 all-gather.11
  597.0 58.4 all-gather.17
  891.9 36.5 all-gather.13
  1052.8 58.4 all-gather.19
where the time goes:
time: 1210 us; the launch traced here: 1200 us
  waiting for transfers between devices  471 us (39%)
  other arithmetic  427 us (35%)
  local copies, waits for them, and re-layouts  165 us (14%)
  starting transfers between devices  58.1 us (5%)
  matrix products  53.8 us (4%)
  between operations  24.2 us (2%)
    another operation x46, other arithmetic, factor_whole(): pivot_factor = jnp.linalg.cholesky(symmetric_lower(corner))  238 us
    ppermute x8, waiting for transfers between devices, partner(): return lax.ppermute(block, axis, route)  178 us
    all_gather x3, waiting for transfers between devices, from_root(): lax.all_gather(array, axis)  157 us
    another operation x7, other arithmetic, factor_whole(): lax.linalg.triangular_solve(pivot_factor, pivot_wide[block_size:], left_s...  119 us
    all_to_all x2, waiting for transfers between devices, shards(): lax.all_to_all(packed, ('row', 'col'), split_axis=0, concat_axis=0, tiled...  89.3 us
    all_to_all x3, waiting for transfers between devices, copy_for_each(): return lax.all_to_all(copies, axis, split_axis=0, concat_axis=0, tiled=True)  46.1 us
    all_to_all x3, starting transfers between devices, copy_for_each(): return lax.all_to_all(copies, axis, split_axis=0, concat_axis=0, tiled=True)  36.3 us
    another operation x21, matrix products, factor_whole(): lax.linalg.triangular_solve(pivot_factor, pivot_wide[block_size:], left_s...  33.5 us
  transfers between devices with their start and end apart: 19, of which 13 were waited for; matrix products, arithmetic and copies ran while one was open for 38% of the time, Pallas kernels for 0%

commit v1 on v0

v1 whole, which is shorter than its diff:
```python
import jax
import jax.numpy as jnp
from jax import lax
from jax.experimental import pallas as pl
from jax.experimental.pallas import tpu as pltpu
from jax.sharding import PartitionSpec as P

side = 4
tile = 8


def dot(left, right, dims=((1,), (0,))):
    return lax.dot_general(
        left,
        right,
        (dims, ((), ())),
        precision=lax.Precision.HIGHEST,
        preferred_element_type=jnp.float32,
    )


def halves(array):
    top = array.astype(jnp.bfloat16)
    return top, (array - top.astype(jnp.float32)).astype(jnp.bfloat16)


def dot_rows(left, right):
    dims = (((1,), (1,)), ((), ()))

    def one(a, b):
        return lax.dot_general(a, b, dims, preferred_element_type=jnp.float32)

    return one(left[0], right[0]) + (one(left[0], right[1]) + one(left[1], right[0]))


def params():
    return pltpu.CompilerParams(vmem_limit_bytes=48 * 2**20)


def vmem():
    return pl.BlockSpec(memory_space=pltpu.VMEM)


def smem():
    return pl.BlockSpec(memory_space=pltpu.SMEM)


def blocks(count, size):
    return jax.ShapeDtypeStruct((count, size, size), jnp.float32)


def low(t, u):
    return t * (t + 1) // 2 + u


def pick(conditions, values, default):
    out = default
    for condition, value in zip(conditions, values):
        out = jnp.where(condition, value, out)
    return out


def shift_of(meta, base, count):
    shift = [meta[base + t] for t in range(count)]
    kind = [s & (side - 1) for s in shift]
    place = []
    for t in range(count):
        place.append(sum([(kind[t] == kind[x]).astype(jnp.int32) for x in range(t)], jnp.int32(0)))
    return shift, kind, place


def run_in_slot(kind, place, want_kind, want_place):
    count = len(kind)
    return pick(
        [(kind[t] == want_kind) & (place[t] == want_place) for t in range(count)],
        range(count),
        jnp.int32(-1),
    )


def parent_rows(shift, mine, count):
    home = []
    for t in range(count):
        origin = (mine - shift[t]) & (side - 1)
        home.append((4 * t + origin + shift[t]) >> 2)
    return [
        pick([home[t] == row for t in range(count)], range(count), jnp.int32(-1))
        for row in range(count + 1)
    ]


def factor_block(block):
    n = block.shape[0]
    groups = [block[tile * i : tile * (i + 1), :] for i in range(n // tile)]
    lane = lax.broadcasted_iota(jnp.int32, (tile, n), 1)
    row_id = lax.broadcasted_iota(jnp.int32, (tile, n), 0)
    lane_one = lax.broadcasted_iota(jnp.int32, (1, n), 1)
    pivots = []
    for g in range(n // tile):
        base = tile * g
        cols = [
            [
                jnp.broadcast_to(groups[i][:, base + k : base + k + 1], (tile, n))
                for i in range(g, n // tile)
            ]
            for k in range(tile)
        ]
        in_panel = jnp.logical_and(lane >= base, lane < base + tile)
        for i in range(g + 1, n // tile):
            groups[i] = jnp.where(in_panel, 0.0, groups[i])
        own = groups[g]
        pivot = jnp.ones((tile, n), jnp.float32)
        for k in range(tile):
            value = cols[k][0][k : k + 1, :]
            pivot = jnp.where(row_id == k, value, pivot)
            scale = 1.0 / value
            row = jnp.where(lane_one == base + k, 1.0, own[k : k + 1, :])
            row_below = jnp.where(
                jnp.logical_and(lane_one > base + k, lane_one < base + tile), 0.0, row
            )
            ratio = jnp.where(row_id > k, cols[k][0] * scale, 0.0)
            for later in range(k + 1, tile):
                cols[later][0] = cols[later][0] - ratio * cols[later][0][k : k + 1, :]
            own = (
                jnp.where(jnp.logical_and(lane == base + k, row_id > k), 0.0, own) - ratio * row
            )
            for x in range(1, n // tile - g):
                ratio = cols[k][x] * scale
                for later in range(k + 1, tile):
                    cols[later][x] = cols[later][x] - ratio * cols[later][0][k : k + 1, :]
                groups[g + x] = groups[g + x] - ratio * row_below
        groups[g] = own
        pivots.append(pivot)
    upper, inverse = [], []
    for g in range(n // tile):
        scale = lax.rsqrt(pivots[g])
        rows = row_id + tile * g
        upper.append(
            jnp.where(lane > rows, groups[g], jnp.where(lane == rows, pivots[g], 0.0)) * scale
        )
        inverse.append(
            jnp.where(lane < rows, groups[g], jnp.where(lane == rows, 1.0, 0.0)) * scale
        )
    return jnp.concatenate(upper, 0), jnp.concatenate(inverse, 0)


def factor_in_place(work, lower, inverse_t, size):
    count = work.shape[0] // size
    order = work.shape[0]
    lower[...] = jnp.zeros_like(lower)
    inverse_t[...] = jnp.zeros_like(inverse_t)

    def step(b, carry):
        at = pl.ds(pl.multiple_of(b * size, size), size)
        upper, inverse = factor_block(work[at, at])
        lower[at, at] = upper.T
        work[at, at] = jnp.eye(size, dtype=jnp.float32)
        wide = dot(inverse, work[at, :])
        work[at, :] = wide

        def rest(c, inner):
            there = pl.ds(pl.multiple_of(c * size, size), size)
            part = work[at, there].T
            lower[there, at] = part
            work[there, at] = jnp.zeros((size, size), jnp.float32)
            work[there, :] -= dot(part, work[at, :])
            return inner

        lax.fori_loop(b + 1, count, rest, 0)

        def save(c, inner):
            there = pl.ds(pl.multiple_of(c * size, size), size)
            inverse_t[there, at] = work[at, there].T
            return inner

        lax.fori_loop(0, b + 1, save, 0)
        return carry

    lax.fori_loop(0, count, step, 0)


def corner_body(meta, q0, q1, q2, q3, block_out, inverse_out, full, work, lower):
    size = block_out.shape[0]
    my_row, my_col = meta[0], meta[1]
    for back_row, ref in enumerate((q0, q1, q2, q3)):
        at_row = pl.ds(pl.multiple_of(((my_row - back_row) & 3) * size, size), size)
        for back_col in range(side):
            at_col = pl.ds(pl.multiple_of(((my_col - back_col) & 3) * size, size), size)
            full[at_row, at_col] = ref[back_col]
    rows = lax.broadcasted_iota(jnp.int32, (size, size), 0)
    cols = lax.broadcasted_iota(jnp.int32, (size, size), 1)
    work[...] = jnp.zeros_like(work)
    for b in range(side):
        at = slice(b * size, (b + 1) * size)
        for c in range(b, side):
            there = slice(c * size, (c + 1) * size)
            block = full[there, at]
            work[at, there] = jnp.where(rows >= cols, block, block.T) if b == c else block.T
    factor_in_place(work, lower, inverse_out, size)
    at_row = pl.ds(pl.multiple_of(my_row * size, size), size)
    at_col = pl.ds(pl.multiple_of(my_col * size, size), size)
    block_out[...] = lower[at_row, at_col]


def factor_corner(meta, quads):
    size = quads[0].shape[-1]
    order = side * size
    return pl.pallas_call(
        corner_body,
        in_specs=[smem()] + [vmem()] * 4,
        out_specs=[vmem()] * 2,
        out_shape=(
            jax.ShapeDtypeStruct((size, size), jnp.float32),
            jax.ShapeDtypeStruct((order, order), jnp.float32),
        ),
        scratch_shapes=[pltpu.VMEM((order, order), jnp.float32)] * 3,
        compiler_params=params(),
        cost_estimate=pl.CostEstimate(flops=3 * 10**9, bytes_accessed=8 * 10**7, transcendentals=0),
        name="factor_corner",
    )(meta, *quads)


def update_body(where, meta, r0, r1, r2, r3, c0, c1, c2, c3, inverse_t, front, panel, update, rows, cols):
    count, size = panel.shape[0], panel.shape[1]
    my_row, my_col = meta[0], meta[1]
    for back in range(side):
        at_col = pl.ds(pl.multiple_of(((my_col - back) & 3) * size, size), size)
        at_row = pl.ds(pl.multiple_of(((my_row - back) & 3) * size, size), size)
        for t in range(count):
            here = slice(t * size, (t + 1) * size)
            rows[here, at_col] = (r0, r1, r2, r3)[back][t]
            cols[here, at_row] = (c0, c1, c2, c3)[back][t]
    rows[...] = dot(rows[...], inverse_t[...])
    cols[...] = dot(cols[...], inverse_t[...])
    mine = pl.ds(pl.multiple_of(my_col * size, size), size)
    for t in range(count):
        panel[t] = rows[t * size : (t + 1) * size, mine]
    across = halves(cols[...])
    for t in range(count):
        here = halves(rows[t * size : (t + 1) * size, :])
        end = (t + 1) * size
        product = dot_rows(here, (across[0][:end], across[1][:end]))
        for u in range(t + 1):
            update[low(t, u)] = (
                front[where[low(t, u)]] - product[:, u * size : (u + 1) * size]
            )


def update_call(where, meta, row_parts, col_parts, inverse_t, front):
    count, size = row_parts[0].shape[0], row_parts[0].shape[1]
    order = side * size
    return pl.pallas_call(
        update_body,
        in_specs=[smem()] * 2 + [vmem()] * 10,
        out_specs=[vmem()] * 2,
        out_shape=(blocks(count, size), blocks(low(count, 0), size)),
        scratch_shapes=[pltpu.VMEM((count * size, order), jnp.float32)] * 2,
        compiler_params=params(),
        cost_estimate=pl.CostEstimate(
            flops=8 * 10**9, bytes_accessed=15 * 10**6, transcendentals=0
        ),
        name="panel_update",
    )(where, meta, *row_parts, *col_parts, inverse_t, front)


def send_slots(meta, get, slots, send):
    count = 6
    my_row, my_col = meta[0], meta[1]
    _, kind, place = shift_of(meta, 2, count)
    table = [[run_in_slot(kind, place, k, i) for i in range(2)] for k in range(side)]
    for k in range(side):
        for i in range(2):
            t = table[k][i]

            @pl.when(t >= 0)
            def _():
                slots[2 * k + i] = get(t + 1, 0)

    for a in range(side):
        for b in range(side):
            device = ((my_row + a) & 3) * side + ((my_col + b) & 3)
            for i in range(2):
                for j in range(2):
                    t, u = table[a][i], table[b][j]

                    @pl.when((u >= 0) & (t >= u))
                    def _():
                        send[device, 2 * i + j] = get(t + 1, u + 1)


def leaf_body(meta, pattern, front, first, slots, send):
    size = first.shape[1]
    my_row, my_col = meta[0], meta[1]

    def get(t, u):
        keep = pattern[4 * t + my_row, 4 * u + my_col].astype(jnp.float32)
        return keep * front[pl.ds(pl.multiple_of(t * size, size), size), pl.ds(pl.multiple_of(u * size, size), size)]

    first[0] = get(0, 0)
    send_slots(meta, get, slots, send)


def leaf_call(meta, pattern, front, size):
    return pl.pallas_call(
        leaf_body,
        in_specs=[smem()] * 2 + [vmem()],
        out_specs=[vmem()] * 3,
        out_shape=(
            blocks(1, size),
            blocks(2 * side, size),
            jax.ShapeDtypeStruct((side * side, 4, size, size), jnp.float32),
        ),
        compiler_params=params(),
        cost_estimate=pl.CostEstimate(flops=10**6, bytes_accessed=8 * 10**6, transcendentals=0),
        name="leaf_pack",
    )(meta, pattern, front)


def merged_blocks(maps, pattern, own, other, share_a, share_b, diag_a, diag_b):
    count = 6
    size = own.shape[1]
    my_row, my_col = maps[0], maps[1]
    tables = []
    for base in (2, 2 + count):
        shift, _, _ = shift_of(maps, base, count)
        tables.append((parent_rows(shift, my_row, count), parent_rows(shift, my_col, count)))
    same = lax.broadcasted_iota(jnp.int32, (size, size), 0) == lax.broadcasted_iota(
        jnp.int32, (size, size), 1
    )

    def fill(t, u, target, index):
        keep = pattern[4 * t + my_row, 4 * u + my_col].astype(jnp.float32)
        if u == 0:
            target[index] = keep * (share_a[t] + share_b[t])
        else:
            target[index] = jnp.zeros((size, size), jnp.float32)
        if t == u:

            @pl.when(my_row == my_col)
            def _():
                entries = diag_a[t : t + 1, :] + diag_b[t : t + 1, :]
                target[index] += jnp.where(same, keep * entries, 0.0)

        for (to_row, to_col), source in zip(tables, (own, other)):
            x, y = to_row[t], to_col[u]

            @pl.when((y >= 0) & (x >= y))
            def _():
                target[index] += source[(x * (x + 1) >> 1) + y]

    return fill


def merge_body(maps, meta, pattern, own, other, share_a, share_b, diag_a, diag_b, first, slots, send, front):
    fill = merged_blocks(maps, pattern, own, other, share_a, share_b, diag_a, diag_b)
    for t in range(7):
        for u in range(t + 1):
            fill(t, u, front, low(t, u))
    first[0] = front[0]

    def get(t, u):
        return front[(t * (t + 1) >> 1) + u]

    send_slots(meta, get, slots, send)


def merge_call(maps, meta, pattern, own, other, share_a, share_b, diag_a, diag_b):
    size = own.shape[1]
    return pl.pallas_call(
        merge_body,
        in_specs=[smem()] * 3 + [vmem()] * 6,
        out_specs=[vmem()] * 3,
        out_shape=(
            blocks(1, size),
            blocks(2 * side, size),
            jax.ShapeDtypeStruct((side * side, 4, size, size), jnp.float32),
        ),
        scratch_shapes=[pltpu.VMEM((28, size, size), jnp.float32)],
        compiler_params=params(),
        cost_estimate=pl.CostEstimate(flops=10**6, bytes_accessed=10**7, transcendentals=0),
        name="merge_pack",
    )(maps, meta, pattern, own, other, share_a, share_b, diag_a, diag_b)


def merge_last_body(maps, pattern, own, other, share_a, share_b, diag_a, diag_b, first, column, front):
    fill = merged_blocks(maps, pattern, own, other, share_a, share_b, diag_a, diag_b)
    fill(0, 0, first, 0)
    for t in range(1, 7):
        fill(t, 0, column, t - 1)
        for u in range(1, t + 1):
            fill(t, u, front, low(t - 1, u - 1))


def merge_last_call(maps, pattern, own, other, share_a, share_b, diag_a, diag_b):
    size = own.shape[1]
    return pl.pallas_call(
        merge_last_body,
        in_specs=[smem()] * 2 + [vmem()] * 6,
        out_specs=[vmem()] * 3,
        out_shape=(blocks(1, size), blocks(6, size), blocks(21, size)),
        compiler_params=params(),
        cost_estimate=pl.CostEstimate(flops=10**6, bytes_accessed=10**7, transcendentals=0),
        name="merge_last",
    )(maps, pattern, own, other, share_a, share_b, diag_a, diag_b)


def settle_body(meta, s0, s1, s2, s3, out):
    count = out.shape[0]
    _, kind, place = shift_of(meta, 2, count)
    for t in range(count):
        for k, ref in enumerate((s0, s1, s2, s3)):

            @pl.when(kind[t] == k)
            def _():
                out[t] = ref[place[t]]


def settle_call(meta, parts, count):
    size = parts[0].shape[1]
    return pl.pallas_call(
        settle_body,
        in_specs=[smem()] + [vmem()] * 4,
        out_specs=vmem(),
        out_shape=blocks(count, size),
        compiler_params=params(),
        name="settle",
    )(meta, *parts)


def slots_body(meta, column, slots):
    _, kind, place = shift_of(meta, 2, column.shape[0])
    for t in range(column.shape[0]):
        slots[2 * kind[t] + place[t]] = column[t]


def slots_call(meta, column):
    return pl.pallas_call(
        slots_body,
        in_specs=[smem(), vmem()],
        out_specs=vmem(),
        out_shape=blocks(2 * side, column.shape[1]),
        compiler_params=params(),
        name="slots",
    )(meta, column)


def rotate(array, axis, by):
    return lax.ppermute(array, axis, [(i, (i + by) % side) for i in range(side)])


def transpose_grid(array):
    route = [(i * side + j, j * side + i) for i in range(side) for j in range(side)]
    return lax.ppermute(array, ("row", "col"), route)


def across(array, bit):
    count = lax.axis_size("leaf")
    return lax.ppermute(array, "leaf", [(i, i ^ (1 << bit)) for i in range(count)])


def around(array, axis):
    return [array] + [rotate(array, axis, k) for k in range(1, side)]


def corner_parts(first):
    strip = jnp.concatenate(around(first, "col"), 0)
    return around(strip, "row")


def shift_slots(slots, sign):
    parts = [slots[2 * k : 2 * k + 2] for k in range(side)]
    return [parts[0]] + [rotate(parts[k], "row", sign * k) for k in range(1, side)]


def shards(leaf_front, leaf_pattern, parent_panel, parent_diag, parent_pattern, ext_map):
    block_rows = leaf_front.shape[1]
    size = leaf_front.shape[3]
    count = block_rows - 1
    levels = parent_panel.shape[0]
    my_row = lax.axis_index("row").astype(jnp.int32)
    my_col = lax.axis_index("col").astype(jnp.int32)
    my_leaf = lax.axis_index("leaf")
    here = jnp.stack([my_row, my_col])
    runs = ext_map.reshape(levels, -1, count, side)[..., 0] - side * jnp.arange(count, dtype=jnp.int32)

    def shift_row(depth, node):
        return lax.dynamic_index_in_dim(runs[depth], node, 0, keepdims=False)

    metas, maps, wheres = [], [], []
    for depth in range(levels):
        node = jnp.right_shift(my_leaf, depth)
        own = shift_row(depth, node)
        metas.append(jnp.concatenate([here, own]))
        maps.append(jnp.concatenate([here, own, shift_row(depth, node ^ 1)]))
        kind = own % side
        ids = jnp.arange(count)
        place = jnp.sum(
            ((kind[:, None] == kind[None, :]) & (ids[:, None] > ids[None, :])).astype(jnp.int32), 1
        )
        from_row = (my_row - own) % side
        from_col = (my_col - own) % side
        table = (from_row[:, None] * side + from_col[None, :]) * 4 + 2 * place[:, None] + place[None, :]
        wheres.append(jnp.concatenate([table[t, : t + 1] for t in range(count)]))
    wheres.append(jnp.arange(low(count, 0), dtype=jnp.int32))
    metas.append(jnp.concatenate([here, jnp.zeros((count,), jnp.int32)]))
    patterns = [leaf_pattern[0]] + [
        lax.dynamic_index_in_dim(
            parent_pattern[depth], jnp.right_shift(my_leaf, depth + 1), 0, keepdims=False
        )
        for depth in range(levels)
    ]

    share = parent_panel.reshape(levels, block_rows, size, size)
    diag = parent_diag.reshape(levels, block_rows, size)
    pairs = []
    for depth in range(levels):
        other_share, other_diag = across((share, diag), depth)
        pairs.append((share[0], other_share[0], diag[0], other_diag[0]))
        if depth + 1 < levels:
            share, diag = share[1:] + other_share[1:], diag[1:] + other_diag[1:]

    panel_list = []
    first, slots, send = leaf_call(
        metas[0], patterns[0], leaf_front.reshape(block_rows * size, block_rows * size), size
    )
    column = None
    for level in range(levels + 1):
        quads = corner_parts(first)
        if level < levels:
            front = lax.all_to_all(send, ("row", "col"), split_axis=0, concat_axis=0, tiled=True)
            front = front.reshape(-1, size, size)
            column = settle_call(metas[level], shift_slots(slots, 1), count)
        row_parts = around(column, "col")
        col_parts = around(transpose_grid(column), "row")
        top, inverse_t = factor_corner(metas[level], quads)
        panel, update = update_call(
            wheres[level], metas[level], row_parts, col_parts, inverse_t, front
        )
        if level < levels:
            other = across(update, level)
            args = (maps[level], metas[level + 1], patterns[level + 1], update, other) + pairs[level]
            if level + 1 < levels:
                first, slots, send = merge_call(*args)
            else:
                first, column, front = merge_last_call(args[0], *args[2:])
            panel = settle_call(
                metas[level], shift_slots(slots_call(metas[level], panel), -1), count
            )
        panel_list.append(jnp.concatenate([top[None], panel], 0))
    panels = jnp.stack(panel_list).reshape(levels + 1, 1, block_rows, 1, size, 1, size)
    ids = jnp.arange(size)
    rows = []
    for t in range(count):
        line = []
        for u in range(count):
            if t < u:
                line.append(jnp.zeros((size, size), jnp.float32))
            elif t == u:
                keep = (my_row * size + ids)[:, None] >= (my_col * size + ids)[None, :]
                line.append(jnp.where(keep, update[low(t, u)], 0.0))
            else:
                line.append(update[low(t, u)])
        rows.append(jnp.stack(line, 1))
    top_update = jnp.stack(rows).reshape(1, count, 1, size, count, 1, size)
    return (panels, top_update)


def solution(mesh):
    return jax.shard_map(
        shards,
        mesh=mesh,
        in_specs=(
            P("leaf", None, "row", None, None, "col", None),
            P("leaf", None, None),
            P(None, "leaf", None, "row", None, "col", None),
            P(None, "leaf", None, "row", None),
            P(),
            P(),
        ),
        out_specs=(
            P(None, "leaf", None, "row", None, "col", None),
            P("leaf", None, "row", None, None, "col", None),
        ),
        check_vma=False,
    )
```

time: 1210 us -> 535 us (0.44)
  other arithmetic: 427 us -> 15.4 us
  waiting for transfers between devices: 471 us -> 230 us
  local copies, waits for them, and re-layouts: 165 us -> 43.5 us
  Pallas kernels: 0 us -> 112 us
  starting transfers between devices: 58.1 us -> 123 us
  matrix products: 53.8 us -> 0 us
  between operations: 24.2 us -> 1.67 us
    another operation x54 -> x5, other arithmetic: 360 us -> 1.38 us  [the longest x4 1.28 us: shards(): jnp.stack(panel_list).reshape(levels + 1, 1, block_rows, 1, size, 1, size)]
    all_gather x6 -> x0, waiting for transfers between devices: 157 us -> none  [the longest x3 157 us: from_root(): lax.all_gather(array, axis)]
    all_to_all x5 -> x2, waiting for transfers between devices: 135 us -> 0.01 us  [shards(): lax.all_to_all(send, ('row', 'col'), split_axis=0, concat_axis=0, tiled=T...]
    pallas_call x0 -> x15, Pallas kernels: none -> 112 us  [the longest x3 64.6 us: factor_corner(): pl.pallas_call(corner_body, in_specs=[smem()] + [vmem()] * 4, out_specs=[...]
    ppermute x8 -> x57, starting transfers between devices: 10.7 us -> 107 us  [the longest x48 86.8 us: rotate(): lax.ppermute(array, axis, [(i, (i + by) % side) for i in range(side)])]
    ppermute x8 -> x57, waiting for transfers between devices: 178 us -> 230 us  [the longest x48 126 us: rotate(): lax.ppermute(array, axis, [(i, (i + by) % side) for i in range(side)])]
    another operation x39 -> x0, matrix products: 40 us -> none  [the longest x21 33.5 us: factor_whole(): lax.linalg.triangular_solve(pivot_factor, pivot_wide[block_size:], left_s...]
    all_to_all x5 -> x2, starting transfers between devices: 46.4 us -> 15.2 us  [shards(): lax.all_to_all(send, ('row', 'col'), split_axis=0, concat_axis=0, tiled=T...]
  transfers between devices with their start and end apart: 19 -> 59, of which waited for: 13 -> 13; matrix products, arithmetic and copies ran while one was open for 38% -> 1% of each run, Pallas kernels for 0% -> 16%
where the time goes in v1:
time: 535 us; the launch traced here: 525 us
  waiting for transfers between devices  230 us (43%)
  starting transfers between devices  123 us (23%)
  Pallas kernels  112 us (21%)
  local copies, waits for them, and re-layouts  43.5 us (8%)
  other arithmetic  15.4 us (3%)
    ppermute x48, waiting for transfers between devices, rotate(): lax.ppermute(array, axis, [(i, (i + by) % side) for i in range(side)])  126 us
    ppermute x6, waiting for transfers between devices, across(): lax.ppermute(array, 'leaf', [(i, i ^ 1 << bit) for i in range(count)])  102 us
    ppermute x48, starting transfers between devices, rotate(): lax.ppermute(array, axis, [(i, (i + by) % side) for i in range(side)])  86.8 us
    pallas_call x3, Pallas kernels, factor_corner(): pl.pallas_call(corner_body, in_specs=[smem()] + [vmem()] * 4, out_specs=[...  64.6 us
    unnamed x114, local copies, waits for them, and re-layouts  36.9 us
    pallas_call x3, Pallas kernels, update_call(): pl.pallas_call(update_body, in_specs=[smem()] * 2 + [vmem()] * 10, out_sp...  32.5 us
    all_to_all x2, starting transfers between devices, shards(): lax.all_to_all(send, ('row', 'col'), split_axis=0, concat_axis=0, tiled=T...  15.2 us
    ppermute x3, starting transfers between devices, transpose_grid(): return lax.ppermute(array, ('row', 'col'), route)  11.7 us
  transfers between devices with their start and end apart: 59, of which 13 were waited for; matrix products, arithmetic and copies ran while one was open for 1% of the time, Pallas kernels for 16%

profile of v1, /device:TPU:1, one launch (start us, length us, event | category | flops | bytes accessed | tf_op | source)
XLA Modules:
  0.0 525.0 jit_solution(10576179895408630581)
XLA Ops:
  2.3 11.4 %reduce.1 = f32[7,128,7,128]{3,2,1,0:T(8,128)} reduce(f32[1,7,1,128,7,1,128]{6,5,4,3,2,1,0:T(1,128)} %param.6, f32[]{:T(128)} %constant.101), dimensions={0,2,5}, to_apply=%param.6.reduce_sub_computation | reduce | bytes 6422532 | tf_op args[0]
  13.7 2.8 copy.68
  16.5 1.1 dynamic-slice_reduce_fusion.2
  17.6 3.8 leaf_pack.1
  22.2 8.6 %all-to-all-start = ((f32[16,4,128,128]{3,2,1,0:T(8,128)}), f32[16,4,128,128]{3,2,1,0:T(8,128)}, u32[]{:S(2)}, u32[]{:S(2)}) async-start(f32[16,4,128,128]{3,2,1,0:T(8,128)} %get-tuple-element.27), calls=%async_computation | async-start | bytes 8388608 | tf_op jit(solution)/shard_map/all_to_all | solution.py:530
  30.8 2.7 collective-permute-start.2
  33.5 1.0 collective-permute-start.1
  35.1 1.3 collective-permute-start.8
  36.4 2.7 collective-permute-start.7
  39.4 45.2 %collective-permute-done = f32[1,128,128]{2,1,0:T(8,128)S(1)} collective-permute-done((f32[1,128,128]{2,1,0:T(8,128)S(1)}, f32[1,128,128]{2,1,0:T(8,128)S(1)}, u32[]{:S(2)}, u32[]{:S(2)}) %collective-permute-start) | collective-permute-done | bytes 65568 | tf_op jit(solution)/shard_map/ppermute | solution.py:448
  84.6 3.0 collective-permute-start.6
  88.3 3.4 collective-permute-start.3
  92.4 3.7 collective-permute-start.12
  96.1 5.1 collective-permute-start.11
  103.3 1.2 collective-permute-done.12.c0
  104.5 2.8 collective-permute-start.15
  108.0 7.7 %collective-permute-start.14 = (f32[6,128,128]{2,1,0:T(8,128)S(1)}, f32[6,128,128]{2,1,0:T(8,128)S(1)}, u32[]{:S(2)}, u32[]{:S(2)}) collective-permute-start(f32[6,128,128]{2,1,0:T(8,128)S(1)} %collective-permute-done.12.c0), channel_id=1, source_target_pairs={{0,8},{4,12},{8,0},{12,4},{1,9},{5,13},{9,1},{13,5},{2,10},{6,14},... | collective-permute-start | bytes 1179656 | tf_op jit(solution)/shard_map/ppermute | solution.py:448
  115.6 10.3 %collective-permute-done.11.r3 = f32[6,128,128]{2,1,0:T(8,128)S(1)} collective-permute-done((f32[6,128,128]{2,1,0:T(8,128)S(1)}, f32[6,128,128]{2,1,0:T(8,128)S(1)}, u32[]{:S(2)}, u32[]{:S(2)}) %collective-permute-start.11) | collective-permute-done | bytes 393248 | tf_op jit(solution)/shard_map/ppermute | solution.py:448
  130.1 21.5 %factor_corner.3 = (f32[128,128]{1,0:T(8,128)S(1)}, f32[512,512]{1,0:T(8,128)S(1)}) custom-call(s32[8]{0:T(128)S(1)} %pad_add_fusion.meta, f32[4,128,128]{2,1,0:T(8,128)S(1)} %constant_dynamic-update-slice_fusion.q0, f32[4,128,128]{2,1,0:T(8,128)S(1)} %copy-done.30, f32[4,128,128]{2,1,0:T(8,128)S(1)} %copy-done.24, f32[4,128,128]{2,1,0:T(8,128)S(1)} %copy-done.22), custom_call_target="tpu_custom_call" | custom-call | flops 3000000000 | bytes 80000000 | tf_op jit(solution)/shard_map/factor_corner/pallas_call | solution.py:208
  152.6 1.6 collective-permute-start.21
  154.4 1.2 copy-done.34
  155.6 11.0 %panel_update.3 = (f32[6,128,128]{2,1,0:T(8,128)S(1)}, f32[21,128,128]{2,1,0:T(8,128)S(1)}) custom-call(s32[21]{0:T(128)S(1)} %concatenate.46.where, s32[8]{0:T(128)S(1)} %pad_add_fusion.meta, f32[6,128,128]{2,1,0:T(8,128)S(1)} %settle.4.r0, f32[6,128,128]{2,1,0:T(8,128)S(1)} %collective-permute-done.9.r1, f32[6,128,128]{2,1,0:T(8,128)S(1)} %collective-permute-done.10.r2, ...), custom_call_target="tpu_custom_call" | custom-call | flops 8000000000 | bytes 15000000 | tf_op jit(solution)/shard_map/panel_update/pallas_call | solution.py:252
  166.6 1.5 collective-permute-start.19
  168.8 1.1 slice_bitcast_fusion.2.share_a
  170.0 5.6 %collective-permute-done.20 = f32[2,7,128,128]{3,2,1,0:T(8,128)} collective-permute-done((f32[2,7,128,128]{3,2,1,0:T(8,128)}, f32[2,7,128,128]{3,2,1,0:T(8,128)}, u32[]{:S(2)}, u32[]{:S(2)}) %collective-permute-start.20) | collective-permute-done | bytes 917536 | tf_op jit(solution)/shard_map/ppermute | solution.py:458
  175.7 1.4 slice_add_fusion
  177.0 28.0 %collective-permute-done.19.other = f32[21,128,128]{2,1,0:T(8,128)S(1)} collective-permute-done((f32[21,128,128]{2,1,0:T(8,128)S(1)}, f32[21,128,128]{2,1,0:T(8,128)S(1)}, u32[]{:S(2)}, u32[]{:S(2)}) %collective-permute-start.19) | collective-permute-done | bytes 1376288 | tf_op jit(solution)/shard_map/ppermute | solution.py:458
  205.0 4.5 merge_pack.1
  209.6 6.7 %all-to-all-start.1 = ((f32[16,4,128,128]{3,2,1,0:T(8,128)}), f32[16,4,128,128]{3,2,1,0:T(8,128)}, u32[]{:S(2)}, u32[]{:S(2)}) async-start(f32[16,4,128,128]{3,2,1,0:T(8,128)} %get-tuple-element.34), calls=%async_computation.1 | async-start | bytes 8388608 | tf_op jit(solution)/shard_map/all_to_all | solution.py:530
  216.5 2.7 collective-permute-start.24
  220.8 1.3 collective-permute-start.30
  222.0 2.7 collective-permute-start.29
  224.7 45.3 %collective-permute-done.22 = f32[1,128,128]{2,1,0:T(8,128)S(1)} collective-permute-done((f32[1,128,128]{2,1,0:T(8,128)S(1)}, f32[1,128,128]{2,1,0:T(8,128)S(1)}, u32[]{:S(2)}, u32[]{:S(2)}) %collective-permute-start.22) | collective-permute-done | bytes 65568 | tf_op jit(solution)/shard_map/ppermute | solution.py:448
  270.0 3.0 collective-permute-start.28
  273.7 3.4 collective-permute-start.25
  277.9 3.7 collective-permute-start.34
  281.5 5.1 collective-permute-start.33
  288.7 1.2 collective-permute-done.34.c0
  289.9 2.8 collective-permute-start.37
  293.4 7.7 %collective-permute-start.36 = (f32[6,128,128]{2,1,0:T(8,128)S(1)}, f32[6,128,128]{2,1,0:T(8,128)}, u32[]{:S(2)}, u32[]{:S(2)}) collective-permute-start(f32[6,128,128]{2,1,0:T(8,128)S(1)} %collective-permute-done.34.c0), channel_id=1, source_target_pairs={{0,8},{4,12},{8,0},{12,4},{1,9},{5,13},{9,1},{13,5},{2,10},{6,14},... | collective-permute-start | bytes 1179656 | tf_op jit(solution)/shard_map/ppermute | solution.py:448
  301.1 10.3 %collective-permute-done.33.r3 = f32[6,128,128]{2,1,0:T(8,128)S(1)} collective-permute-done((f32[6,128,128]{2,1,0:T(8,128)S(1)}, f32[6,128,128]{2,1,0:T(8,128)S(1)}, u32[]{:S(2)}, u32[]{:S(2)}) %collective-permute-start.33) | collective-permute-done | bytes 393248 | tf_op jit(solution)/shard_map/ppermute | solution.py:448
  315.8 21.5 %factor_corner.4 = (f32[128,128]{1,0:T(8,128)S(1)}, f32[512,512]{1,0:T(8,128)S(1)}) custom-call(s32[8]{0:T(128)S(1)} %pad_add_fusion.2.meta, f32[4,128,128]{2,1,0:T(8,128)S(1)} %constant_dynamic-update-slice_fusion.4.q0, f32[4,128,128]{2,1,0:T(8,128)S(1)} %copy-done.32, f32[4,128,128]{2,1,0:T(8,128)S(1)} %copy-done.28, f32[4,128,128]{2,1,0:T(8,128)S(1)} %copy-done.26), custom_call_target="tpu_custom_call" | custom-call | flops 3000000000 | bytes 80000000 | tf_op jit(solution)/shard_map/factor_corner/pallas_call | solution.py:208
  342.4 1.2 copy-done.36
  343.6 11.2 %panel_update.4 = (f32[6,128,128]{2,1,0:T(8,128)S(1)}, f32[21,128,128]{2,1,0:T(8,128)S(1)}) custom-call(s32[21]{0:T(128)S(1)} %concatenate.51.where, s32[8]{0:T(128)S(1)} %pad_add_fusion.2.meta, f32[6,128,128]{2,1,0:T(8,128)S(1)} %settle.6.r0, f32[6,128,128]{2,1,0:T(8,128)S(1)} %copy-done.18, f32[6,128,128]{2,1,0:T(8,128)S(1)} %collective-permute-done.32.r2, ...), custom_call_target="tpu_custom_call" | custom-call | flops 8000000000 | bytes 15000000 | tf_op jit(solution)/shard_map/panel_update/pallas_call | solution.py:252
  355.6 3.2 collective-permute-start.41
  359.8 2.3 collective-permute-start.42
  363.9 4.2 collective-permute-start.17
  369.7 59.1 %collective-permute-done.43 = f32[1,7,128]{2,1,0:T(8,128)S(1)} collective-permute-done((f32[1,7,128]{2,1,0:T(8,128)S(1)}, f32[1,7,128]{2,1,0:T(8,128)S(1)}, u32[]{:S(2)}, u32[]{:S(2)}) %collective-permute-start.43) | collective-permute-done | bytes 3616 | tf_op jit(solution)/shard_map/ppermute | solution.py:458
  429.4 9.3 %collective-permute-done.42 = f32[1,7,128,128]{3,2,1,0:T(8,128)S(1)} collective-permute-done((f32[1,7,128,128]{3,2,1,0:T(8,128)S(1)}, f32[1,7,128,128]{3,2,1,0:T(8,128)S(1)}, u32[]{:S(2)}, u32[]{:S(2)}) %collective-permute-start.42) | collective-permute-done | bytes 458784 | tf_op jit(solution)/shard_map/ppermute | solution.py:458
  438.7 2.6 merge_last.1
  441.3 1.1 copy-done.16
  442.4 1.4 collective-permute-start.44
  443.8 4.2 collective-permute-done.44
  449.1 3.4 collective-permute-start.39
  454.0 4.3 collective-permute-start.53
  458.3 3.5 collective-permute-start.52
  463.9 2.4 collective-permute-start.47
  471.5 6.0 %collective-permute-done.49.q3 = f32[4,128,128]{2,1,0:T(8,128)S(1)} collective-permute-done((f32[4,128,128]{2,1,0:T(8,128)S(1)}, f32[4,128,128]{2,1,0:T(8,128)S(1)}, u32[]{:S(2)}, u32[]{:S(2)}) %collective-permute-start.49) | collective-permute-done | bytes 262176 | tf_op jit(solution)/shard_map/ppermute | solution.py:448
  478.0 4.9 collective-permute-start.56
  482.9 4.1 collective-permute-done.52.r3
  487.1 21.6 %factor_corner.5 = (f32[128,128]{1,0:T(8,128)S(1)}, f32[512,512]{1,0:T(8,128)S(1)}) custom-call(s32[8]{0:T(128)S(1)} %pad_add_fusion.5.meta, f32[4,128,128]{2,1,0:T(8,128)S(1)} %constant_dynamic-update-slice_fusion.8.q0, f32[4,128,128]{2,1,0:T(8,128)S(1)} %collective-permute-done.47.q1, f32[4,128,128]{2,1,0:T(8,128)S(1)} %collective-permute-done.48.q2, ...), custom_call_target="tpu_custom_call" | custom-call | flops 3000000000 | bytes 80000000 | tf_op jit(solution)/shard_map/factor_corner/pallas_call | solution.py:208
  508.8 10.3 %panel_update.5 = (f32[6,128,128]{2,1,0:T(8,128)S(1)}, f32[21,128,128]{2,1,0:T(8,128)S(1)}) custom-call(s32[21]{0:T(128)S(1)} %iota.26.where, s32[8]{0:T(128)S(1)} %pad_add_fusion.5.meta, f32[6,128,128]{2,1,0:T(8,128)} %get-tuple-element.39.r0, f32[6,128,128]{2,1,0:T(8,128)S(1)} %collective-permute-done.50.r1, ...), custom_call_target="tpu_custom_call" | custom-call | flops 8000000000 | bytes 15000000 | tf_op jit(solution)/shard_map/panel_update/pallas_call | solution.py:252
  519.7 3.8 copy.49
  523.6 1.2 pad_maximum_fusion
  (249 shorter events, 45.5 us)
Async XLA Ops:
  17.5 21.5 %copy-start.40 = (s32[6]{0:T(128)}, s32[6]{0:T(128)S(1)}, u32[]{:S(2)}) copy-start(s32[6]{0:T(128)S(1)} %get-tuple-element.108) | copy-start | bytes 76
  22.2 132.1 %all-to-all-start = ((f32[16,4,128,128]{3,2,1,0:T(8,128)}), f32[16,4,128,128]{3,2,1,0:T(8,128)}, u32[]{:S(2)}, u32[]{:S(2)}) async-start(f32[16,4,128,128]{3,2,1,0:T(8,128)} %get-tuple-element.27), calls=%async_computation | async-start | bytes 8388608 | tf_op jit(solution)/shard_map/all_to_all | solution.py:530
  30.8 95.9 %copy-start.38 = (f32[2,1,7,1,128]{4,3,2,1,0:T(1,128)S(1)}, f32[2,1,7,1,128]{4,3,2,1,0:T(1,128)}, u32[]{:S(2)}) copy-start(f32[2,1,7,1,128]{4,3,2,1,0:T(1,128)} %param.9) | copy-start | bytes 21508
  30.8 56.9 %collective-permute-start.2 = (f32[1,128,128]{2,1,0:T(8,128)S(1)}, f32[1,128,128]{2,1,0:T(8,128)S(1)}, u32[]{:S(2)}, u32[]{:S(2)}) collective-permute-start(f32[1,128,128]{2,1,0:T(8,128)S(1)} %get-tuple-element.23), channel_id=1, source_target_pairs={{0,3},{1,0},{2,1},{3,2},{4,7},{5,4},{6,5},{7,6},{8,11},{9,8},{10,9... | collective-permute-start | bytes 196616 | tf_op jit(solution)/shard_map/ppermute | solution.py:448
  33.5 54.2 %collective-permute-start.1 = (f32[1,128,128]{2,1,0:T(8,128)S(1)}, f32[1,128,128]{2,1,0:T(8,128)S(1)}, u32[]{:S(2)}, u32[]{:S(2)}) collective-permute-start(f32[1,128,128]{2,1,0:T(8,128)S(1)} %get-tuple-element.23), channel_id=1, source_target_pairs={{0,2},{1,3},{2,0},{3,1},{4,6},{5,7},{6,4},{7,5},{8,10},{9,11},{10,... | collective-permute-start | bytes 196616 | tf_op jit(solution)/shard_map/ppermute | solution.py:448
  34.5 50.1 %collective-permute-start = (f32[1,128,128]{2,1,0:T(8,128)S(1)}, f32[1,128,128]{2,1,0:T(8,128)S(1)}, u32[]{:S(2)}, u32[]{:S(2)}) collective-permute-start(f32[1,128,128]{2,1,0:T(8,128)S(1)} %get-tuple-element.23), channel_id=1, source_target_pairs={{0,1},{1,2},{2,3},{3,0},{4,5},{5,6},{6,7},{7,4},{8,9},{9,10},{10,1... | collective-permute-start | bytes 196616 | tf_op jit(solution)/shard_map/ppermute | solution.py:448
  35.1 53.2 %collective-permute-start.8 = (f32[2,128,128]{2,1,0:T(8,128)S(1)}, f32[2,128,128]{2,1,0:T(8,128)S(1)}, u32[]{:S(2)}, u32[]{:S(2)}) collective-permute-start(f32[2,128,128]{2,1,0:T(8,128)S(1)} %get-tuple-element.89), channel_id=1, source_target_pairs={{0,12},{4,0},{8,4},{12,8},{1,13},{5,1},{9,5},{13,9},{2,14},{6,2},{... | collective-permute-start | bytes 393224 | tf_op jit(solution)/shard_map/ppermute | solution.py:448
  36.4 55.3 %collective-permute-start.7 = (f32[2,128,128]{2,1,0:T(8,128)S(1)}, f32[2,128,128]{2,1,0:T(8,128)S(1)}, u32[]{:S(2)}, u32[]{:S(2)}) collective-permute-start(f32[2,128,128]{2,1,0:T(8,128)S(1)} %get-tuple-element.90), channel_id=1, source_target_pairs={{0,8},{4,12},{8,0},{12,4},{1,9},{5,13},{9,1},{13,5},{2,10},{6,14},... | collective-permute-start | bytes 393224 | tf_op jit(solution)/shard_map/ppermute | solution.py:448
  84.6 7.1 %collective-permute-start.6 = (f32[2,128,128]{2,1,0:T(8,128)S(1)}, f32[2,128,128]{2,1,0:T(8,128)S(1)}, u32[]{:S(2)}, u32[]{:S(2)}) collective-permute-start(f32[2,128,128]{2,1,0:T(8,128)S(1)} %get-tuple-element.91), channel_id=1, source_target_pairs={{0,4},{4,8},{8,12},{12,0},{1,5},{5,9},{9,13},{13,1},{2,6},{6,10},{... | collective-permute-start | bytes 393224 | tf_op jit(solution)/shard_map/ppermute | solution.py:448
  87.7 13.6 %collective-permute-start.5 = (f32[4,128,128]{2,1,0:T(8,128)S(1)}, f32[4,128,128]{2,1,0:T(8,128)S(1)}, u32[]{:S(2)}, u32[]{:S(2)}) collective-permute-start(f32[4,128,128]{2,1,0:T(8,128)S(1)} %constant_dynamic-update-slice_fusion.q0), channel_id=1, source_target_pairs={{0,12},{4,0},{8,4},{12,8},{1,13},{5,1},{9,5},{13,9},{2,14},{6,2},{... | collective-permute-start | bytes 786440 | tf_op jit(solution)/shard_map/ppermute | solution.py:448
  87.8 14.2 %collective-permute-start.4 = (f32[4,128,128]{2,1,0:T(8,128)S(1)}, f32[4,128,128]{2,1,0:T(8,128)S(1)}, u32[]{:S(2)}, u32[]{:S(2)}) collective-permute-start(f32[4,128,128]{2,1,0:T(8,128)S(1)} %constant_dynamic-update-slice_fusion.q0), channel_id=1, source_target_pairs={{0,8},{4,12},{8,0},{12,4},{1,9},{5,13},{9,1},{13,5},{2,10},{6,14},... | collective-permute-start | bytes 786440 | tf_op jit(solution)/shard_map/ppermute | solution.py:448
  88.3 19.0 %collective-permute-start.3 = (f32[4,128,128]{2,1,0:T(8,128)S(1)}, f32[4,128,128]{2,1,0:T(8,128)S(1)}, u32[]{:S(2)}, u32[]{:S(2)}) collective-permute-start(f32[4,128,128]{2,1,0:T(8,128)S(1)} %constant_dynamic-update-slice_fusion.q0), channel_id=1, source_target_pairs={{0,4},{4,8},{8,12},{12,0},{1,5},{5,9},{9,13},{13,1},{2,6},{6,10},{... | collective-permute-start | bytes 786440 | tf_op jit(solution)/shard_map/ppermute | solution.py:448
  92.4 12.1 %collective-permute-start.12 = (f32[6,128,128]{2,1,0:T(8,128)S(1)}, f32[6,128,128]{2,1,0:T(8,128)S(1)}, u32[]{:S(2)}, u32[]{:S(2)}) collective-permute-start(f32[6,128,128]{2,1,0:T(8,128)S(1)} %settle.4.r0), channel_id=1, source_target_pairs={{0,0},{1,4},{2,8},{3,12},{4,1},{5,5},{6,9},{7,13},{8,2},{9,6},{10,... | collective-permute-start | bytes 1179656 | tf_op jit(solution)/shard_map/ppermute | solution.py:453
  96.1 29.9 %collective-permute-start.11 = (f32[6,128,128]{2,1,0:T(8,128)S(1)}, f32[6,128,128]{2,1,0:T(8,128)S(1)}, u32[]{:S(2)}, u32[]{:S(2)}) collective-permute-start(f32[6,128,128]{2,1,0:T(8,128)S(1)} %settle.4.r0), channel_id=1, source_target_pairs={{0,3},{1,0},{2,1},{3,2},{4,7},{5,4},{6,5},{7,6},{8,11},{9,8},{10,9... | collective-permute-start | bytes 1179656 | tf_op jit(solution)/shard_map/ppermute | solution.py:448
  102.0 50.6 %collective-permute-start.10 = (f32[6,128,128]{2,1,0:T(8,128)S(1)}, f32[6,128,128]{2,1,0:T(8,128)S(1)}, u32[]{:S(2)}, u32[]{:S(2)}) collective-permute-start(f32[6,128,128]{2,1,0:T(8,128)S(1)} %settle.4.r0), channel_id=1, source_target_pairs={{0,2},{1,3},{2,0},{3,1},{4,6},{5,7},{6,4},{7,5},{8,10},{9,11},{10,... | collective-permute-start | bytes 1179656 | tf_op jit(solution)/shard_map/ppermute | solution.py:448
  102.7 51.5 %collective-permute-start.9 = (f32[6,128,128]{2,1,0:T(8,128)S(1)}, f32[6,128,128]{2,1,0:T(8,128)S(1)}, u32[]{:S(2)}, u32[]{:S(2)}) collective-permute-start(f32[6,128,128]{2,1,0:T(8,128)S(1)} %settle.4.r0), channel_id=1, source_target_pairs={{0,1},{1,2},{2,3},{3,0},{4,5},{5,6},{6,7},{7,4},{8,9},{9,10},{10,1... | collective-permute-start | bytes 1179656 | tf_op jit(solution)/shard_map/ppermute | solution.py:448
  104.5 49.8 %collective-permute-start.15 = (f32[6,128,128]{2,1,0:T(8,128)S(1)}, f32[6,128,128]{2,1,0:T(8,128)S(1)}, u32[]{:S(2)}, u32[]{:S(2)}) collective-permute-start(f32[6,128,128]{2,1,0:T(8,128)S(1)} %collective-permute-done.12.c0), channel_id=1, source_target_pairs={{0,12},{4,0},{8,4},{12,8},{1,13},{5,1},{9,5},{13,9},{2,14},{6,2},{... | collective-permute-start | bytes 1179656 | tf_op jit(solution)/shard_map/ppermute | solution.py:448
  108.0 46.3 %collective-permute-start.14 = (f32[6,128,128]{2,1,0:T(8,128)S(1)}, f32[6,128,128]{2,1,0:T(8,128)S(1)}, u32[]{:S(2)}, u32[]{:S(2)}) collective-permute-start(f32[6,128,128]{2,1,0:T(8,128)S(1)} %collective-permute-done.12.c0), channel_id=1, source_target_pairs={{0,8},{4,12},{8,0},{12,4},{1,9},{5,13},{9,1},{13,5},{2,10},{6,14},... | collective-permute-start | bytes 1179656 | tf_op jit(solution)/shard_map/ppermute | solution.py:448
  126.0 28.3 %collective-permute-start.13 = (f32[6,128,128]{2,1,0:T(8,128)S(1)}, f32[6,128,128]{2,1,0:T(8,128)S(1)}, u32[]{:S(2)}, u32[]{:S(2)}) collective-permute-start(f32[6,128,128]{2,1,0:T(8,128)S(1)} %collective-permute-done.12.c0), channel_id=1, source_target_pairs={{0,4},{4,8},{8,12},{12,0},{1,5},{5,9},{9,13},{13,1},{2,6},{6,10},{... | collective-permute-start | bytes 1179656 | tf_op jit(solution)/shard_map/ppermute | solution.py:448
  152.6 17.4 %collective-permute-start.21 = (f32[2,7,128]{2,1,0:T(8,128)S(1)}, f32[2,7,128]{2,1,0:T(8,128)S(1)}, u32[]{:S(2)}, u32[]{:S(2)}) collective-permute-start(f32[2,7,128]{2,1,0:T(8,128)S(1)} %copy.44), channel_id=1, source_target_pairs={{0,16},{16,0},{32,48},{48,32},{64,80},{80,64},{96,112},{112,96},{1... | collective-permute-start | bytes 21512 | tf_op jit(solution)/shard_map/ppermute | solution.py:458
  154.2 21.4 %collective-permute-start.20 = (f32[2,7,128,128]{3,2,1,0:T(8,128)}, f32[2,7,128,128]{3,2,1,0:T(8,128)}, u32[]{:S(2)}, u32[]{:S(2)}) collective-permute-start(f32[2,7,128,128]{3,2,1,0:T(8,128)} %bitcast.16), channel_id=1, source_target_pairs={{0,16},{16,0},{32,48},{48,32},{64,80},{80,64},{96,112},{112,96},{1... | collective-permute-start | bytes 2752520 | tf_op jit(solution)/shard_map/ppermute | solution.py:458
  166.6 43.0 %copy-start.2 = (f32[6,128,128]{2,1,0:T(8,128)}, f32[6,128,128]{2,1,0:T(8,128)S(1)}, u32[]{:S(2)}) copy-start(f32[6,128,128]{2,1,0:T(8,128)S(1)} %get-tuple-element.28.column) | copy-start | bytes 1179652
  166.6 38.5 %collective-permute-start.19 = (f32[21,128,128]{2,1,0:T(8,128)S(1)}, f32[21,128,128]{2,1,0:T(8,128)S(1)}, u32[]{:S(2)}, u32[]{:S(2)}) collective-permute-start(f32[21,128,128]{2,1,0:T(8,128)S(1)} %get-tuple-element.29.own), channel_id=1, source_target_pairs={{0,16},{16,0},{32,48},{48,32},{64,80},{80,64},{96,112},{112,96},{1... | collective-permute-start | bytes 4128776 | tf_op jit(solution)/shard_map/ppermute | solution.py:458
  209.6 130.8 %all-to-all-start.1 = ((f32[16,4,128,128]{3,2,1,0:T(8,128)}), f32[16,4,128,128]{3,2,1,0:T(8,128)}, u32[]{:S(2)}, u32[]{:S(2)}) async-start(f32[16,4,128,128]{3,2,1,0:T(8,128)} %get-tuple-element.34), calls=%async_computation.1 | async-start | bytes 8388608 | tf_op jit(solution)/shard_map/all_to_all | solution.py:530
  216.5 56.6 %collective-permute-start.24 = (f32[1,128,128]{2,1,0:T(8,128)S(1)}, f32[1,128,128]{2,1,0:T(8,128)S(1)}, u32[]{:S(2)}, u32[]{:S(2)}) collective-permute-start(f32[1,128,128]{2,1,0:T(8,128)S(1)} %get-tuple-element.30), channel_id=1, source_target_pairs={{0,3},{1,0},{2,1},{3,2},{4,7},{5,4},{6,5},{7,6},{8,11},{9,8},{10,9... | collective-permute-start | bytes 196616 | tf_op jit(solution)/shard_map/ppermute | solution.py:448
  219.2 53.9 %collective-permute-start.23 = (f32[1,128,128]{2,1,0:T(8,128)S(1)}, f32[1,128,128]{2,1,0:T(8,128)S(1)}, u32[]{:S(2)}, u32[]{:S(2)}) collective-permute-start(f32[1,128,128]{2,1,0:T(8,128)S(1)} %get-tuple-element.30), channel_id=1, source_target_pairs={{0,2},{1,3},{2,0},{3,1},{4,6},{5,7},{6,4},{7,5},{8,10},{9,11},{10,... | collective-permute-start | bytes 196616 | tf_op jit(solution)/shard_map/ppermute | solution.py:448
  219.7 50.3 %collective-permute-start.22 = (f32[1,128,128]{2,1,0:T(8,128)S(1)}, f32[1,128,128]{2,1,0:T(8,128)S(1)}, u32[]{:S(2)}, u32[]{:S(2)}) collective-permute-start(f32[1,128,128]{2,1,0:T(8,128)S(1)} %get-tuple-element.30), channel_id=1, source_target_pairs={{0,1},{1,2},{2,3},{3,0},{4,5},{5,6},{6,7},{7,4},{8,9},{9,10},{10,1... | collective-permute-start | bytes 196616 | tf_op jit(solution)/shard_map/ppermute | solution.py:448
  220.8 53.0 %collective-permute-start.30 = (f32[2,128,128]{2,1,0:T(8,128)S(1)}, f32[2,128,128]{2,1,0:T(8,128)S(1)}, u32[]{:S(2)}, u32[]{:S(2)}) collective-permute-start(f32[2,128,128]{2,1,0:T(8,128)S(1)} %get-tuple-element.85), channel_id=1, source_target_pairs={{0,12},{4,0},{8,4},{12,8},{1,13},{5,1},{9,5},{13,9},{2,14},{6,2},{... | collective-permute-start | bytes 393224 | tf_op jit(solution)/shard_map/ppermute | solution.py:448
  222.0 55.1 %collective-permute-start.29 = (f32[2,128,128]{2,1,0:T(8,128)S(1)}, f32[2,128,128]{2,1,0:T(8,128)S(1)}, u32[]{:S(2)}, u32[]{:S(2)}) collective-permute-start(f32[2,128,128]{2,1,0:T(8,128)S(1)} %get-tuple-element.86), channel_id=1, source_target_pairs={{0,8},{4,12},{8,0},{12,4},{1,9},{5,13},{9,1},{13,5},{2,10},{6,14},... | collective-permute-start | bytes 393224 | tf_op jit(solution)/shard_map/ppermute | solution.py:448
  270.0 7.1 %collective-permute-start.28 = (f32[2,128,128]{2,1,0:T(8,128)S(1)}, f32[2,128,128]{2,1,0:T(8,128)S(1)}, u32[]{:S(2)}, u32[]{:S(2)}) collective-permute-start(f32[2,128,128]{2,1,0:T(8,128)S(1)} %get-tuple-element.87), channel_id=1, source_target_pairs={{0,4},{4,8},{8,12},{12,0},{1,5},{5,9},{9,13},{13,1},{2,6},{6,10},{... | collective-permute-start | bytes 393224 | tf_op jit(solution)/shard_map/ppermute | solution.py:448
  273.1 13.6 %collective-permute-start.27 = (f32[4,128,128]{2,1,0:T(8,128)S(1)}, f32[4,128,128]{2,1,0:T(8,128)S(1)}, u32[]{:S(2)}, u32[]{:S(2)}) collective-permute-start(f32[4,128,128]{2,1,0:T(8,128)S(1)} %constant_dynamic-update-slice_fusion.4.q0), channel_id=1, source_target_pairs={{0,12},{4,0},{8,4},{12,8},{1,13},{5,1},{9,5},{13,9},{2,14},{6,2},{... | collective-permute-start | bytes 786440 | tf_op jit(solution)/shard_map/ppermute | solution.py:448
  273.2 14.2 %collective-permute-start.26 = (f32[4,128,128]{2,1,0:T(8,128)S(1)}, f32[4,128,128]{2,1,0:T(8,128)S(1)}, u32[]{:S(2)}, u32[]{:S(2)}) collective-permute-start(f32[4,128,128]{2,1,0:T(8,128)S(1)} %constant_dynamic-update-slice_fusion.4.q0), channel_id=1, source_target_pairs={{0,8},{4,12},{8,0},{12,4},{1,9},{5,13},{9,1},{13,5},{2,10},{6,14},... | collective-permute-start | bytes 786440 | tf_op jit(solution)/shard_map/ppermute | solution.py:448
  273.7 19.0 %collective-permute-start.25 = (f32[4,128,128]{2,1,0:T(8,128)S(1)}, f32[4,128,128]{2,1,0:T(8,128)S(1)}, u32[]{:S(2)}, u32[]{:S(2)}) collective-permute-start(f32[4,128,128]{2,1,0:T(8,128)S(1)} %constant_dynamic-update-slice_fusion.4.q0), channel_id=1, source_target_pairs={{0,4},{4,8},{8,12},{12,0},{1,5},{5,9},{9,13},{13,1},{2,6},{6,10},{... | collective-permute-start | bytes 786440 | tf_op jit(solution)/shard_map/ppermute | solution.py:448
  277.9 12.1 %collective-permute-start.34 = (f32[6,128,128]{2,1,0:T(8,128)S(1)}, f32[6,128,128]{2,1,0:T(8,128)S(1)}, u32[]{:S(2)}, u32[]{:S(2)}) collective-permute-start(f32[6,128,128]{2,1,0:T(8,128)S(1)} %settle.6.r0), channel_id=1, source_target_pairs={{0,0},{1,4},{2,8},{3,12},{4,1},{5,5},{6,9},{7,13},{8,2},{9,6},{10,... | collective-permute-start | bytes 1179656 | tf_op jit(solution)/shard_map/ppermute | solution.py:453
  281.5 29.9 %collective-permute-start.33 = (f32[6,128,128]{2,1,0:T(8,128)S(1)}, f32[6,128,128]{2,1,0:T(8,128)S(1)}, u32[]{:S(2)}, u32[]{:S(2)}) collective-permute-start(f32[6,128,128]{2,1,0:T(8,128)S(1)} %settle.6.r0), channel_id=1, source_target_pairs={{0,3},{1,0},{2,1},{3,2},{4,7},{5,4},{6,5},{7,6},{8,11},{9,8},{10,9... | collective-permute-start | bytes 1179656 | tf_op jit(solution)/shard_map/ppermute | solution.py:448
  287.4 51.4 %collective-permute-start.32 = (f32[6,128,128]{2,1,0:T(8,128)S(1)}, f32[6,128,128]{2,1,0:T(8,128)S(1)}, u32[]{:S(2)}, u32[]{:S(2)}) collective-permute-start(f32[6,128,128]{2,1,0:T(8,128)S(1)} %settle.6.r0), channel_id=1, source_target_pairs={{0,2},{1,3},{2,0},{3,1},{4,6},{5,7},{6,4},{7,5},{8,10},{9,11},{10,... | collective-permute-start | bytes 1179656 | tf_op jit(solution)/shard_map/ppermute | solution.py:448
  288.1 50.7 %collective-permute-start.31 = (f32[6,128,128]{2,1,0:T(8,128)S(1)}, f32[6,128,128]{2,1,0:T(8,128)S(1)}, u32[]{:S(2)}, u32[]{:S(2)}) collective-permute-start(f32[6,128,128]{2,1,0:T(8,128)S(1)} %settle.6.r0), channel_id=1, source_target_pairs={{0,1},{1,2},{2,3},{3,0},{4,5},{5,6},{6,7},{7,4},{8,9},{9,10},{10,1... | collective-permute-start | bytes 1179656 | tf_op jit(solution)/shard_map/ppermute | solution.py:448
  289.9 49.7 %collective-permute-start.37 = (f32[6,128,128]{2,1,0:T(8,128)S(1)}, f32[6,128,128]{2,1,0:T(8,128)S(1)}, u32[]{:S(2)}, u32[]{:S(2)}) collective-permute-start(f32[6,128,128]{2,1,0:T(8,128)S(1)} %collective-permute-done.34.c0), channel_id=1, source_target_pairs={{0,12},{4,0},{8,4},{12,8},{1,13},{5,1},{9,5},{13,9},{2,14},{6,2},{... | collective-permute-start | bytes 1179656 | tf_op jit(solution)/shard_map/ppermute | solution.py:448
  293.4 46.9 %collective-permute-start.36 = (f32[6,128,128]{2,1,0:T(8,128)S(1)}, f32[6,128,128]{2,1,0:T(8,128)}, u32[]{:S(2)}, u32[]{:S(2)}) collective-permute-start(f32[6,128,128]{2,1,0:T(8,128)S(1)} %collective-permute-done.34.c0), channel_id=1, source_target_pairs={{0,8},{4,12},{8,0},{12,4},{1,9},{5,13},{9,1},{13,5},{2,10},{6,14},... | collective-permute-start | bytes 1179656 | tf_op jit(solution)/shard_map/ppermute | solution.py:448
  311.4 28.9 %collective-permute-start.35 = (f32[6,128,128]{2,1,0:T(8,128)S(1)}, f32[6,128,128]{2,1,0:T(8,128)}, u32[]{:S(2)}, u32[]{:S(2)}) collective-permute-start(f32[6,128,128]{2,1,0:T(8,128)S(1)} %collective-permute-done.34.c0), channel_id=1, source_target_pairs={{0,4},{4,8},{8,12},{12,0},{1,5},{5,9},{9,13},{13,1},{2,6},{6,10},{... | collective-permute-start | bytes 1179656 | tf_op jit(solution)/shard_map/ppermute | solution.py:448
  343.6 16.1 %copy-start.42 = (s32[6]{0:T(128)S(1)}, s32[6]{0:T(128)}, u32[]{:S(2)}) copy-start(s32[6]{0:T(128)} %get-tuple-element.55) | copy-start | bytes 76
  355.6 83.1 %collective-permute-start.41 = (f32[21,128,128]{2,1,0:T(8,128)S(1)}, f32[21,128,128]{2,1,0:T(8,128)S(1)}, u32[]{:S(2)}, u32[]{:S(2)}) collective-permute-start(f32[21,128,128]{2,1,0:T(8,128)S(1)} %get-tuple-element.36.own), channel_id=1, source_target_pairs={{0,32},{16,48},{32,0},{48,16},{64,96},{80,112},{96,64},{112,80},{1... | collective-permute-start | bytes 4128776 | tf_op jit(solution)/shard_map/ppermute | solution.py:458
  359.8 69.1 %collective-permute-start.43 = (f32[1,7,128]{2,1,0:T(8,128)S(1)}, f32[1,7,128]{2,1,0:T(8,128)S(1)}, u32[]{:S(2)}, u32[]{:S(2)}) collective-permute-start(f32[1,7,128]{2,1,0:T(8,128)S(1)} %get-tuple-element.95), channel_id=1, source_target_pairs={{0,32},{16,48},{32,0},{48,16},{64,96},{80,112},{96,64},{112,80},{1... | collective-permute-start | bytes 10760 | tf_op jit(solution)/shard_map/ppermute | solution.py:458
  359.8 78.8 %collective-permute-start.42 = (f32[1,7,128,128]{3,2,1,0:T(8,128)S(1)}, f32[1,7,128,128]{3,2,1,0:T(8,128)S(1)}, u32[]{:S(2)}, u32[]{:S(2)}) collective-permute-start(f32[1,7,128,128]{3,2,1,0:T(8,128)S(1)} %get-tuple-element.75), channel_id=1, source_target_pairs={{0,32},{16,48},{32,0},{48,16},{64,96},{80,112},{96,64},{112,80},{1... | collective-permute-start | bytes 1376264 | tf_op jit(solution)/shard_map/ppermute | solution.py:458
  363.8 84.6 %collective-permute-start.18 = (f32[2,128,128]{2,1,0:T(8,128)S(1)}, f32[2,128,128]{2,1,0:T(8,128)S(1)}, u32[]{:S(2)}, u32[]{:S(2)}) collective-permute-start(f32[2,128,128]{2,1,0:T(8,128)S(1)} %get-tuple-element.77), channel_id=1, source_target_pairs={{0,4},{4,8},{8,12},{12,0},{1,5},{5,9},{9,13},{13,1},{2,6},{6,10},{... | collective-permute-start | bytes 393224 | tf_op jit(solution)/shard_map/ppermute | solution.py:448
  363.9 88.6 %collective-permute-start.17 = (f32[2,128,128]{2,1,0:T(8,128)S(1)}, f32[2,128,128]{2,1,0:T(8,128)S(1)}, u32[]{:S(2)}, u32[]{:S(2)}) collective-permute-start(f32[2,128,128]{2,1,0:T(8,128)S(1)} %get-tuple-element.78), channel_id=1, source_target_pairs={{0,8},{4,12},{8,0},{12,4},{1,9},{5,13},{9,1},{13,5},{2,10},{6,14},... | collective-permute-start | bytes 393224 | tf_op jit(solution)/shard_map/ppermute | solution.py:448
  428.8 25.1 %collective-permute-start.16 = (f32[2,128,128]{2,1,0:T(8,128)S(1)}, f32[2,128,128]{2,1,0:T(8,128)S(1)}, u32[]{:S(2)}, u32[]{:S(2)}) collective-permute-start(f32[2,128,128]{2,1,0:T(8,128)S(1)} %get-tuple-element.79), channel_id=1, source_target_pairs={{0,12},{4,0},{8,4},{12,8},{1,13},{5,1},{9,5},{13,9},{2,14},{6,2},{... | collective-permute-start | bytes 393224 | tf_op jit(solution)/shard_map/ppermute | solution.py:448
  438.7 23.2 %collective-permute-start.40 = (f32[2,128,128]{2,1,0:T(8,128)S(1)}, f32[2,128,128]{2,1,0:T(8,128)S(1)}, u32[]{:S(2)}, u32[]{:S(2)}) collective-permute-start(f32[2,128,128]{2,1,0:T(8,128)S(1)} %get-tuple-element.81), channel_id=1, source_target_pairs={{0,4},{4,8},{8,12},{12,0},{1,5},{5,9},{9,13},{13,1},{2,6},{6,10},{... | collective-permute-start | bytes 393224 | tf_op jit(solution)/shard_map/ppermute | solution.py:448
  442.4 44.7 %copy-start.15 = (f32[128,128]{1,0:T(8,128)S(1)}, f32[128,128]{1,0:T(8,128)}, u32[]{:S(2)}) copy-start(f32[128,128]{1,0:T(8,128)} %copy-done.14) | copy-start | bytes 196612
  442.4 5.6 %collective-permute-start.44 = (f32[1,128,128]{2,1,0:T(8,128)S(1)}, f32[1,128,128]{2,1,0:T(8,128)S(1)}, u32[]{:S(2)}, u32[]{:S(2)}) collective-permute-start(f32[1,128,128]{2,1,0:T(8,128)S(1)} %get-tuple-element.37), channel_id=1, source_target_pairs={{0,1},{1,2},{2,3},{3,0},{4,5},{5,6},{6,7},{7,4},{8,9},{9,10},{10,1... | collective-permute-start | bytes 196616 | tf_op jit(solution)/shard_map/ppermute | solution.py:448
  447.9 5.2 collective-permute-start.45
  449.1 13.9 %collective-permute-start.39 = (f32[2,128,128]{2,1,0:T(8,128)S(1)}, f32[2,128,128]{2,1,0:T(8,128)S(1)}, u32[]{:S(2)}, u32[]{:S(2)}) collective-permute-start(f32[2,128,128]{2,1,0:T(8,128)S(1)} %get-tuple-element.82), channel_id=1, source_target_pairs={{0,8},{4,12},{8,0},{12,4},{1,9},{5,13},{9,1},{13,5},{2,10},{6,14},... | collective-permute-start | bytes 393224 | tf_op jit(solution)/shard_map/ppermute | solution.py:448
  453.1 10.8 %collective-permute-start.38 = (f32[2,128,128]{2,1,0:T(8,128)S(1)}, f32[2,128,128]{2,1,0:T(8,128)S(1)}, u32[]{:S(2)}, u32[]{:S(2)}) collective-permute-start(f32[2,128,128]{2,1,0:T(8,128)S(1)} %get-tuple-element.83), channel_id=1, source_target_pairs={{0,12},{4,0},{8,4},{12,8},{1,13},{5,1},{9,5},{13,9},{2,14},{6,2},{... | collective-permute-start | bytes 393224 | tf_op jit(solution)/shard_map/ppermute | solution.py:448
  453.1 5.2 collective-permute-start.46
  454.0 24.0 %collective-permute-start.53 = (f32[6,128,128]{2,1,0:T(8,128)}, f32[6,128,128]{2,1,0:T(8,128)S(1)}, u32[]{:S(2)}, u32[]{:S(2)}) collective-permute-start(f32[6,128,128]{2,1,0:T(8,128)} %get-tuple-element.39.r0), channel_id=1, source_target_pairs={{0,0},{1,4},{2,8},{3,12},{4,1},{5,5},{6,9},{7,13},{8,2},{9,6},{10,... | collective-permute-start | bytes 1179656 | tf_op jit(solution)/shard_map/ppermute | solution.py:453
  458.3 28.7 %collective-permute-start.52 = (f32[6,128,128]{2,1,0:T(8,128)}, f32[6,128,128]{2,1,0:T(8,128)S(1)}, u32[]{:S(2)}, u32[]{:S(2)}) collective-permute-start(f32[6,128,128]{2,1,0:T(8,128)} %get-tuple-element.39.r0), channel_id=1, source_target_pairs={{0,3},{1,0},{2,1},{3,2},{4,7},{5,4},{6,5},{7,6},{8,11},{9,8},{10,9... | collective-permute-start | bytes 1179656 | tf_op jit(solution)/shard_map/ppermute | solution.py:448
  462.5 14.9 %collective-permute-start.49 = (f32[4,128,128]{2,1,0:T(8,128)S(1)}, f32[4,128,128]{2,1,0:T(8,128)S(1)}, u32[]{:S(2)}, u32[]{:S(2)}) collective-permute-start(f32[4,128,128]{2,1,0:T(8,128)S(1)} %constant_dynamic-update-slice_fusion.8.q0), channel_id=1, source_target_pairs={{0,12},{4,0},{8,4},{12,8},{1,13},{5,1},{9,5},{13,9},{2,14},{6,2},{... | collective-permute-start | bytes 786440 | tf_op jit(solution)/shard_map/ppermute | solution.py:448
  463.0 14.9 %collective-permute-start.48 = (f32[4,128,128]{2,1,0:T(8,128)S(1)}, f32[4,128,128]{2,1,0:T(8,128)S(1)}, u32[]{:S(2)}, u32[]{:S(2)}) collective-permute-start(f32[4,128,128]{2,1,0:T(8,128)S(1)} %constant_dynamic-update-slice_fusion.8.q0), channel_id=1, source_target_pairs={{0,8},{4,12},{8,0},{12,4},{1,9},{5,13},{9,1},{13,5},{2,10},{6,14},... | collective-permute-start | bytes 786440 | tf_op jit(solution)/shard_map/ppermute | solution.py:448
  463.9 19.0 %collective-permute-start.47 = (f32[4,128,128]{2,1,0:T(8,128)S(1)}, f32[4,128,128]{2,1,0:T(8,128)S(1)}, u32[]{:S(2)}, u32[]{:S(2)}) collective-permute-start(f32[4,128,128]{2,1,0:T(8,128)S(1)} %constant_dynamic-update-slice_fusion.8.q0), channel_id=1, source_target_pairs={{0,4},{4,8},{8,12},{12,0},{1,5},{5,9},{9,13},{13,1},{2,6},{6,10},{... | collective-permute-start | bytes 786440 | tf_op jit(solution)/shard_map/ppermute | solution.py:448
  477.5 31.2 %collective-permute-start.51 = (f32[6,128,128]{2,1,0:T(8,128)}, f32[6,128,128]{2,1,0:T(8,128)S(1)}, u32[]{:S(2)}, u32[]{:S(2)}) collective-permute-start(f32[6,128,128]{2,1,0:T(8,128)} %get-tuple-element.39.r0), channel_id=1, source_target_pairs={{0,2},{1,3},{2,0},{3,1},{4,6},{5,7},{6,4},{7,5},{8,10},{9,11},{10,... | collective-permute-start | bytes 1179656 | tf_op jit(solution)/shard_map/ppermute | solution.py:448
  477.9 30.8 %collective-permute-start.50 = (f32[6,128,128]{2,1,0:T(8,128)}, f32[6,128,128]{2,1,0:T(8,128)S(1)}, u32[]{:S(2)}, u32[]{:S(2)}) collective-permute-start(f32[6,128,128]{2,1,0:T(8,128)} %get-tuple-element.39.r0), channel_id=1, source_target_pairs={{0,1},{1,2},{2,3},{3,0},{4,5},{5,6},{6,7},{7,4},{8,9},{9,10},{10,1... | collective-permute-start | bytes 1179656 | tf_op jit(solution)/shard_map/ppermute | solution.py:448
  478.0 30.7 %collective-permute-start.56 = (f32[6,128,128]{2,1,0:T(8,128)S(1)}, f32[6,128,128]{2,1,0:T(8,128)S(1)}, u32[]{:S(2)}, u32[]{:S(2)}) collective-permute-start(f32[6,128,128]{2,1,0:T(8,128)S(1)} %collective-permute-done.53.c0), channel_id=1, source_target_pairs={{0,12},{4,0},{8,4},{12,8},{1,13},{5,1},{9,5},{13,9},{2,14},{6,2},{... | collective-permute-start | bytes 1179656 | tf_op jit(solution)/shard_map/ppermute | solution.py:448
  482.9 25.8 %collective-permute-start.55 = (f32[6,128,128]{2,1,0:T(8,128)S(1)}, f32[6,128,128]{2,1,0:T(8,128)S(1)}, u32[]{:S(2)}, u32[]{:S(2)}) collective-permute-start(f32[6,128,128]{2,1,0:T(8,128)S(1)} %collective-permute-done.53.c0), channel_id=1, source_target_pairs={{0,8},{4,12},{8,0},{12,4},{1,9},{5,13},{9,1},{13,5},{2,10},{6,14},... | collective-permute-start | bytes 1179656 | tf_op jit(solution)/shard_map/ppermute | solution.py:448
  487.0 21.7 %collective-permute-start.54 = (f32[6,128,128]{2,1,0:T(8,128)S(1)}, f32[6,128,128]{2,1,0:T(8,128)S(1)}, u32[]{:S(2)}, u32[]{:S(2)}) collective-permute-start(f32[6,128,128]{2,1,0:T(8,128)S(1)} %collective-permute-done.53.c0), channel_id=1, source_target_pairs={{0,4},{4,8},{8,12},{12,0},{1,5},{5,9},{9,13},{13,1},{2,6},{6,10},{... | collective-permute-start | bytes 1179656 | tf_op jit(solution)/shard_map/ppermute | solution.py:448
  (39 other events, 103.8 us)
